TPU v7x, 128 devices: a whole 4x4x4 slice. The times are simulated.
128 devices in a mesh: section: 16 (over x_hi, y, core), dp: 8 (over x_lo, z).
Axes of the slice: x: 4 (x_hi: 2, x_lo: 2; x = x_hi * 2 + x_lo), y: 4, z: 4, core: 2. Of those that a mesh axis runs over, the one named last changes fastest.
Arguments:
- master_weights: float32 [16, 8192, 512], P('section', 'dp'), may hold values from -0.0625 to 0.0625
- first_moment: float32 [16, 8192, 512], P('section', 'dp'), may hold values from -2 to 2
- second_moment: float32 [16, 8192, 512], P('section', 'dp'), may hold values from 0.05 to 2
- gradient_shard: float32 [16, 8192, 512], P('section', 'dp'), may hold values from -6 to 6
- hidden_states: bfloat16 [16, 2, 1024, 8192], P('section', None, 'dp'), may hold values from -6 to 6
Outputs:
- new_master: float32 [16, 8192, 512], P('section', 'dp')
- new_first: float32 [16, 8192, 512], P('section', 'dp')
- new_second: float32 [16, 8192, 512], P('section', 'dp')
- hidden_out: bfloat16 [16, 2, 1024, 8192], P('section', None, 'dp')
All inputs are finite; a program needn't handle non-finite values.
Results may differ from a plain program's by a relative error of at most 0.008.
Values may be sent and summed in bfloat16 or wider, within the bound.
No kernel may reach another device: no remote copies, remote signals or barrier semaphores. Data moves between devices by JAX's collectives and lax.ppermute only.
A program may use at most 192 MiB of HBM per device.

v0:
```python
import dataclasses
import functools

import jax
import jax.numpy as jnp
from jax import lax
from jax.experimental import pallas as pl
from jax.experimental.pallas import tpu as pltpu
from jax.sharding import PartitionSpec as P

ADAM_STEP = 1000

beta_one = 0.9
beta_two = 0.95
learn_rate = 0.0003
decay_rate = 0.1
adam_eps = 1e-08
norm_eps = 1e-05

AXES = ("section", "dp")
D = 8192
KVW = 512
ROWS = 256
SUB = 512
HALF = D // 2
LANES = 128
VMEM = 56 * 1024 * 1024
UPDATE_STEPS = 4
SUB_STEP = SUB // UPDATE_STEPS
AHEAD = 3


def place(linear):
    section, dp = divmod(linear, 8)
    return section // 2, section % 2, dp // 4, dp % 4


def linear_of(chip, core, xlo, z):
    return ((chip % 8) * 2 + core) * 8 + (xlo % 2) * 4 + z % 4


def shift(value, move):
    pairs = [(source, linear_of(*move(*place(source)))) for source in range(128)]
    return lax.ppermute(value, AXES, pairs)


def to_core(value):
    return shift(value, lambda chip, core, xlo, z: (chip, 1 - core, xlo, z))


def to_pair(value):
    return shift(value, lambda chip, core, xlo, z: (chip, core, xlo + 1, z))


def to_ring(value):
    return shift(value, lambda chip, core, xlo, z: (chip, core, xlo, z + 1 - 2 * core))


def to_chip(value, steps):
    return shift(value, lambda chip, core, xlo, z: (chip + steps, core, xlo, z))


def to_next(value, hop):
    def move(chip, core, xlo, z):
        xhi, y = divmod(chip, 4)
        start = (y - hop + 2 * hop * core) % 4
        if start >= 2 and hop == ((start + core) % 2):
            xhi = 1 - xhi
        return xhi * 4 + (y + 1 - 2 * core) % 4, core, xlo, z

    return shift(value, move)


def adamw_update(master, moment, second, gradient):
    moment_new = beta_one * moment + (1.0 - beta_one) * gradient
    second_new = beta_two * second + (1.0 - beta_two) * gradient * gradient
    corr_one = 1.0 - beta_one**ADAM_STEP
    corr_two = 1.0 - beta_two**ADAM_STEP
    step_size = moment_new / corr_one / (jnp.sqrt(second_new / corr_two) + adam_eps)
    master_new = master - learn_rate * (step_size + decay_rate * master)
    return (master_new, moment_new, second_new)


def update_kernel(
    core_ref,
    master_ref,
    moment_ref,
    second_ref,
    gradient_ref,
    whole,
    master_out,
    moment_out,
    second_out,
    keep_rows,
    give_rows,
    keep,
    give,
    sems,
):
    step = pl.program_id(0)
    core = core_ref[0]

    def copies():
        for part in range(8):
            for side, target in ((core, keep), (1 - core, give)):
                column = pl.multiple_of(part * 2 * SUB + side * SUB, SUB)
                yield pltpu.make_async_copy(
                    whole.at[:, pl.ds(column, SUB)],
                    target.at[:, pl.ds(part * SUB, SUB)],
                    sems.at[part, 0 if target is keep else 1],
                )

    @pl.when(step == 0)
    def _():
        for copy in copies():
            copy.start()

    new_master, new_moment, new_second = adamw_update(
        master_ref[...], moment_ref[...], second_ref[...], gradient_ref[...]
    )
    master_out[...] = new_master
    moment_out[...] = new_moment
    second_out[...] = new_second
    first = new_master[0].astype(jnp.bfloat16)
    last = new_master[1].astype(jnp.bfloat16)
    keep_rows[...] = jnp.where(core == 0, first, last)
    give_rows[...] = jnp.where(core == 0, last, first)

    @pl.when(step == UPDATE_STEPS - 1)
    def _():
        for copy in copies():
            copy.wait()


def update_call(core, master, moment, second, gradient, whole):
    any_space = pl.BlockSpec(memory_space=pl.ANY)
    state = pl.BlockSpec((2, SUB_STEP, KVW), lambda i, core: (0, i, 0))
    half = pl.BlockSpec((SUB_STEP, KVW), lambda i, core: (i, 0))
    shaped = [a.reshape(2, SUB, KVW) for a in (master, moment, second, gradient)]
    outs = pl.pallas_call(
        update_kernel,
        grid_spec=pltpu.PrefetchScalarGridSpec(
            num_scalar_prefetch=1,
            grid=(UPDATE_STEPS,),
            in_specs=[state] * 4 + [any_space],
            out_specs=[state] * 3 + [half] * 2 + [any_space] * 2,
            scratch_shapes=[pltpu.SemaphoreType.DMA((8, 2))],
        ),
        out_shape=[jax.ShapeDtypeStruct((2, SUB, KVW), jnp.float32)] * 3
        + [jax.ShapeDtypeStruct((SUB, KVW), jnp.bfloat16)] * 2
        + [jax.ShapeDtypeStruct((ROWS, HALF), jnp.bfloat16)] * 2,
        compiler_params=pltpu.CompilerParams(vmem_limit_bytes=VMEM),
        cost_estimate=pl.CostEstimate(flops=0, bytes_accessed=23 << 20, transcendentals=0),
        name="update",
    )(core, *shaped, whole)
    return [a.reshape(master.shape) for a in outs[:3]], *outs[3:]


def read_columns(table, blocks, slots, sems, order):
    copies = {}
    for chunk in order:
        column = pl.multiple_of(table[chunk], SUB)
        for index, block in enumerate(blocks):
            copies[chunk, index] = pltpu.make_async_copy(
                block.at[:, pl.ds(column, SUB)],
                slots.at[chunk, pl.ds(index * ROWS, ROWS)],
                sems.at[chunk, index],
            )
    return copies


def picked_columns(table, arrays, slots, sems, order):
    return {
        (chunk, 0): Picked(
            table[8],
            *(
                read_columns(table, (array,), slots, sems, (chunk,))[chunk, 0]
                for array in arrays
            ),
        )
        for chunk in order
    }


@dataclasses.dataclass(frozen=True)
class Picked:
    core: jax.Array
    lower: object
    upper: object

    def start(self):
        pl.when(self.core == 0)(self.lower.start)
        pl.when(self.core == 1)(self.upper.start)

    def wait(self):
        self.lower.wait()


def chunks_of(pieces):
    return [
        piece.at[pl.ds(start, SUB)] for piece in pieces for start in range(0, piece.shape[0], SUB)
    ]


def read_pieces(pieces, slots, sems):
    return [
        pltpu.make_async_copy(chunk, slots.at[index], sems.at[index])
        for index, chunk in enumerate(chunks_of(pieces))
    ]


def layer_kernel(plan, *refs):
    refs = list(refs)

    def take(count):
        taken, refs[:count] = refs[:count], []
        return taken

    (table,) = take(1)
    blocks = take(plan.blocks + plan.picks)
    mine, theirs = take(2) if plan.last else (None, None)
    last = take(plan.last)
    begun = take(1) if plan.adds else []
    after = take(plan.after)
    fresh = take(plan.blocks) if plan.last else []
    out = take(1) if plan.after else []
    columns, column_sems = take(2)
    last_slots, last_sems = take(2) if plan.last else (None, None)
    after_slots, after_sems = take(2) if plan.after else (None, None)
    (store_sems,) = take(1) if plan.last else (None,)

    taken_up = range(plan.first, plan.first + plan.count)
    chunks = range(8) if plan.last else taken_up
    read = picked_columns if plan.picks else read_columns
    reads = read(table, blocks, columns, column_sems, chunks)
    last_reads = read_pieces(last, last_slots, last_sems) if plan.last else []
    after_reads = read_pieces(after, after_slots, after_sems) if plan.after else []

    def begin(chunk):
        if chunk not in chunks:
            return
        for index in range(plan.blocks):
            reads[chunk, index].start()
        if plan.last:
            last_reads[chunk].start()
        if chunk in taken_up:
            after_reads[chunk - plan.first].start()

    for ahead in range(AHEAD):
        begin(chunks[0] + ahead)
    rows = plan.blocks * ROWS
    if plan.last:
        summed = mine[...] + theirs[...]
        scale = lax.rsqrt(summed[:, KVW : KVW + 1] * (1.0 / D) + norm_eps)
        projected = (summed[:, :KVW] * scale).astype(jnp.bfloat16)
    skip = plan.skip * ROWS
    if plan.after:
        total = jnp.zeros((rows - skip, KVW), jnp.float32)
        squares = jnp.zeros((rows - skip, 1), jnp.float32)
        if plan.adds:
            total += begun[0][:, :KVW]
            squares += begun[0][:, KVW : KVW + 1]
    stores = []
    for chunk in chunks:
        begin(chunk + AHEAD)
        for index in range(plan.blocks):
            reads[chunk, index].wait()
        part = columns[chunk]
        if plan.last:
            last_reads[chunk].wait()
            update = lax.dot_general(
                projected,
                last_slots[chunk],
                (((1,), (1,)), ((), ())),
                preferred_element_type=jnp.float32,
            )
            part = (part.astype(jnp.float32) + update).astype(jnp.bfloat16)
            columns[chunk] = part
            column = pl.multiple_of(table[chunk], SUB)
            if plan.swaps:
                own = table[8]
                sources = [own * ROWS, (1 - own) * ROWS]
            else:
                sources = [index * ROWS for index in range(plan.blocks)]
            for index in range(plan.blocks):
                stores.append(
                    pltpu.make_async_copy(
                        columns.at[chunk, pl.ds(sources[index], ROWS)],
                        fresh[index].at[:, pl.ds(column, SUB)],
                        store_sems.at[chunk, index],
                    )
                )
                stores[-1].start()
        if chunk in taken_up:
            after_reads[chunk - plan.first].wait()
            part = part[skip:]
            total += jnp.dot(
                part,
                after_slots[chunk - plan.first],
                preferred_element_type=jnp.float32,
            )
            flat = part.astype(jnp.float32)
            squares += jnp.sum(flat * flat, axis=1, keepdims=True)
    if plan.after:
        out[0][:, :KVW] = total
        out[0][:, KVW:] = jnp.broadcast_to(squares, (rows - skip, LANES))
    for store in stores:
        store.wait()


@dataclasses.dataclass(frozen=True)
class Plan:
    blocks: int
    last: int
    after: int
    first: int = 0
    count: int = 0
    adds: bool = False
    skip: int = 0
    swaps: bool = False
    picks: bool = False


def layer_call(table, blocks, sums=(), last=(), begun=(), after=(), name="layer", **plan):
    count = sum(piece.shape[0] for piece in after) // SUB
    picks = plan.get("picks", False)
    plan = Plan(len(blocks) - picks, len(last), len(after), count=count, adds=len(begun) > 0, **plan)
    rows = plan.blocks * ROWS
    any_space = pl.BlockSpec(memory_space=pl.ANY)
    vmem = pl.BlockSpec(memory_space=pltpu.VMEM)
    out_shape, out_specs = [], []
    scratch = [
        pltpu.VMEM((8, rows, SUB), jnp.bfloat16),
        pltpu.SemaphoreType.DMA((8, plan.blocks)),
    ]
    if plan.last:
        out_shape += [jax.ShapeDtypeStruct((ROWS, HALF), jnp.bfloat16)] * plan.blocks
        out_specs += [any_space] * plan.blocks
        scratch += [pltpu.VMEM((8, SUB, KVW), jnp.bfloat16), pltpu.SemaphoreType.DMA((8,))]
    if plan.after:
        out_shape.append(jax.ShapeDtypeStruct((rows - plan.skip * ROWS, KVW + LANES), jnp.float32))
        out_specs.append(vmem)
        scratch += [
            pltpu.VMEM((plan.count, SUB, KVW), jnp.bfloat16),
            pltpu.SemaphoreType.DMA((plan.count,)),
        ]
    if plan.last:
        scratch.append(pltpu.SemaphoreType.DMA((8, plan.blocks)))
    flops = 2 * SUB * KVW * (rows * 8 * (plan.last > 0) + (rows - plan.skip * ROWS) * count)
    moved = (2 << 20) * plan.blocks * (1 + (plan.last > 0)) + (4 << 20) * (plan.last > 0)
    moved += count << 19
    return pl.pallas_call(
        functools.partial(layer_kernel, plan),
        in_specs=[pl.BlockSpec(memory_space=pltpu.SMEM)]
        + [any_space] * len(blocks)
        + [vmem] * len(sums)
        + [any_space] * len(last)
        + [vmem] * len(begun)
        + [any_space] * len(after),
        out_specs=out_specs,
        out_shape=out_shape,
        scratch_shapes=scratch,
        compiler_params=pltpu.CompilerParams(vmem_limit_bytes=VMEM),
        cost_estimate=pl.CostEstimate(flops=flops, bytes_accessed=moved, transcendentals=0),
        name=name,
    )(table, *blocks, *sums, *last, *begun, *after)


def final_kernel(table, keep, got, mine, theirs, *refs):
    pieces, (whole, slots, slot_sems, w_slots, w_sems, store_sems) = refs[:-6], refs[-6:]
    upper = table[8] == 1
    reads, stores = [], []
    for chunk in range(16):
        source = keep if chunk < 8 else got
        column = pl.multiple_of(table[(0 if chunk < 8 else 16) + chunk % 8], SUB)
        reads.append(
            pltpu.make_async_copy(
                source.at[:, pl.ds(column, SUB)], slots.at[chunk], slot_sems.at[chunk]
            )
        )
        side = table[8] if chunk < 8 else 1 - table[8]
        target = pl.multiple_of(2 * column + side * SUB, SUB)
        stores.append(
            pltpu.make_async_copy(
                slots.at[chunk], whole.at[:, pl.ds(target, SUB)], store_sems.at[chunk]
            )
        )
    weights = read_pieces(pieces, w_slots, w_sems)

    def begin(chunk):
        if chunk < 16:
            reads[chunk].start()
            weights[chunk].start()

    for ahead in range(2 * AHEAD):
        begin(ahead)
    summed = mine[...] + theirs[...]
    scale = lax.rsqrt(summed[:, KVW : KVW + 1] * (1.0 / D) + norm_eps)
    projected = (summed[:, :KVW] * scale).astype(jnp.bfloat16)
    for chunk in range(16):
        begin(chunk + 2 * AHEAD)
        reads[chunk].wait()
        weights[chunk].wait()

        @pl.when(upper)
        def _():
            update = lax.dot_general(
                projected,
                w_slots[chunk],
                (((1,), (1,)), ((), ())),
                preferred_element_type=jnp.float32,
            )
            slots[chunk] = (slots[chunk].astype(jnp.float32) + update).astype(jnp.bfloat16)

        stores[chunk].start()
    for store in stores:
        store.wait()


def final_call(table, keep, got, mine, theirs, here, there):
    any_space = pl.BlockSpec(memory_space=pl.ANY)
    vmem = pl.BlockSpec(memory_space=pltpu.VMEM)
    return pl.pallas_call(
        final_kernel,
        in_specs=[pl.BlockSpec(memory_space=pltpu.SMEM), any_space, any_space, vmem, vmem]
        + [any_space] * (len(here) + len(there)),
        out_specs=any_space,
        out_shape=jax.ShapeDtypeStruct((ROWS, D), jnp.bfloat16),
        scratch_shapes=[
            pltpu.VMEM((16, ROWS, SUB), jnp.bfloat16),
            pltpu.SemaphoreType.DMA((16,)),
            pltpu.VMEM((16, SUB, KVW), jnp.bfloat16),
            pltpu.SemaphoreType.DMA((16,)),
            pltpu.SemaphoreType.DMA((16,)),
        ],
        compiler_params=pltpu.CompilerParams(vmem_limit_bytes=VMEM),
        cost_estimate=pl.CostEstimate(
            flops=2 * ROWS * D * KVW, bytes_accessed=16 << 20, transcendentals=0
        ),
        name="final_layer",
    )(table, keep, got, mine, theirs, *here, *there)


def after(value, *events):
    return lax.optimization_barrier((value, *events))[0]


def together(own, other):
    return jnp.concatenate([own, other], axis=0)


def per_device(master_weights, first_moment, second_moment, gradient_shard, hidden_states):
    core = lax.rem(lax.axis_index("section"), 2)
    xlo = lax.div(lax.axis_index("dp"), 4)
    z = lax.rem(lax.axis_index("dp"), 4)
    upper = core == 1
    core_word = jnp.reshape(core, (1,)).astype(jnp.int32)
    step = jnp.arange(4, dtype=jnp.int32)

    def columns(is_upper):
        owner = lax.rem(z + jnp.where(is_upper, step, 4 - step), 4)
        return jnp.stack([owner + 4 * xlo, owner + 4 * (1 - xlo)], axis=1).reshape(8) * SUB

    filler = jnp.zeros((7,), jnp.int32)
    table = jnp.concatenate([columns(upper), core_word, filler, columns(~upper)]).astype(jnp.int32)

    states, mine, theirs, keep, give = update_call(
        core_word,
        master_weights,
        first_moment,
        second_moment,
        gradient_shard,
        hidden_states.reshape(ROWS, D),
    )
    other = to_core(theirs)
    even_rows = jnp.where(upper, other, mine)
    odd_rows = jnp.where(upper, mine, other)
    got = to_core(after(give, other))

    home_own = [even_rows, to_ring(even_rows)]
    home_other = to_pair(even_rows)
    near_odd = to_chip(odd_rows, 1)
    odd = to_next(jnp.where(upper, keep, got), 0)

    phase = (home_own[1], home_other, near_odd)
    home_own.append(to_ring(after(home_own[1], *phase)))
    home_others = [after(home_other, *phase)]
    home_others.append(to_ring(home_others[0]))
    far = to_chip(after(near_odd, *phase), 1)
    near_even = to_chip(after(even_rows, *phase), 1)

    phase = (home_own[2], home_others[1], far)
    home_own.append(to_ring(after(home_own[2], *phase)))
    home_others.append(to_ring(after(home_others[1], *phase)))
    far = after(far, *phase)
    far_other = to_pair(far)

    phase = (home_own[3], home_others[2], far_other, odd)
    home_others.append(to_ring(after(home_others[2], *phase)))
    first = [after(together(far, far_other), *phase)]
    first.append(to_ring(first[0]))
    odd = to_next(after(odd, *phase), 1)

    home = [piece for pair in zip(home_own, home_others) for piece in pair]
    (product,) = layer_call(table, (keep, got), after=home, picks=True, name="project_home")
    phase = (first[1], home_others[3], near_even)
    first.append(to_ring(after(first[1], *phase)))
    second_own = [after(near_even, *phase)]
    second_own.append(to_ring(second_own[0]))
    second_others = [to_pair(second_own[0])]
    (even,) = layer_call(
        table,
        (keep, got),
        sums=(product, to_core(after(product, *phase))),
        last=home,
        picks=True,
        name="expand_home",
    )
    even = to_next(even, 0)
    third_other = to_pair(after(near_odd, even))

    phase = (first[2], second_own[1], odd)
    first.append(to_ring(after(first[2], *phase)))
    second_own.append(to_ring(after(second_own[1], *phase)))
    second_others.append(to_pair(second_own[1]))
    home_there = to_core(jnp.concatenate([after(piece, *phase) for piece in home], axis=0))

    phase = (first[3], second_own[2], even, third_other, second_others[0])
    even = to_next(after(even, *phase), 1)
    third = [after(together(near_odd, third_other), *phase)]
    third.append(to_ring(third[0]))
    second_own.append(to_ring(after(second_own[2], *phase)))
    second_others.append(to_pair(after(second_own[2], *phase)))

    phase = (third[1], second_own[3], home_there, second_others[1])
    third.append(to_ring(after(third[1], *phase)))
    second_others.append(to_pair(after(second_own[3], *phase)))
    second = [piece for pair in zip(second_own, second_others) for piece in pair]
    even = after(even, *phase, second_others[2])
    third.append(to_ring(third[2]))

    (product,) = layer_call(table, (even, odd), after=first, name="project_first")
    even, odd, product = layer_call(
        table,
        (even, odd),
        sums=(product, to_core(product)),
        last=first,
        after=second,
        name="first_second",
    )
    even, odd, product = layer_call(
        table,
        (even, odd),
        sums=(product, to_core(product)),
        last=second,
        after=third[:3],
        name="second_third",
    )
    (product,) = layer_call(
        table, (even, odd), begun=(product,), after=third[3:], first=6, name="third_rest"
    )
    keep, give, product = layer_call(
        table,
        (even, odd),
        sums=(product, to_core(product)),
        last=third,
        after=home,
        skip=1,
        swaps=True,
        name="third_home",
    )
    out = final_call(
        table, keep, to_core(give), product, to_core(product), home, [home_there]
    )
    return (*states, out.reshape(hidden_states.shape))


def solution(mesh):
    placed = (
        P("section", "dp", None),
        P("section", "dp", None),
        P("section", "dp", None),
        P("section", "dp", None),
        P("section", None, "dp", None),
    )
    return jax.shard_map(
        per_device,
        mesh=mesh,
        in_specs=placed,
        out_specs=(
            P("section", "dp", None),
            P("section", "dp", None),
            P("section", "dp", None),
            P("section", None, "dp", None),
        ),
        check_vma=False,
    )
```

profile of v0, /device:TPU:1, one launch (start us, length us, event | category | flops | bytes accessed | tf_op | source)
XLA Modules:
  0.0 462.9 jit_solution(2550465140855728871)
XLA Ops:
  0.6 131.1 %update.1 = (f32[2,512,512]{2,1,0:T(8,128)}, f32[2,512,512]{2,1,0:T(8,128)}, f32[2,512,512]{2,1,0:T(8,128)}, bf16[512,512]{1,0:T(8,128)(2,1)}, bf16[512,512]{1,0...) custom-call(s32[1]{0:T(128)} %bitcast.core_ref, f32[2,512,512]{2,1,0:T(8,128)} %bitcast.12, ...), custom_call_target="tpu_custom_call" | custom-call | bytes 24117248 | tf_op jit(solution)/shard_map/update/pallas_call | solution.py:140
  131.7 1.5 collective-permute-start
  133.2 1.7 collective-permute-done
  135.3 4.0 collective-permute-done.1.refs_2_
  139.3 2.6 broadcast_select_fusion
  141.9 2.9 collective-permute-start.11
  144.9 1.3 collective-permute-start.2
  146.2 3.8 collective-permute-start.3
  150.0 7.4 %collective-permute-done.2.refs_4_.refs_6_.refs_10_.refs_1_ = bf16[512,512]{1,0:T(8,128)(2,1)S(1)} collective-permute-done((bf16[512,512]{1,0:T(8,128)(2,1)S(1)}, bf16[512,512]{1,0:T(8,128)(2,1)S(1)}, u32[]{:S(2)}, u32[]{:S(2)}) %collective-permute-start.2) | collective-permute-done | bytes 524320 | tf_op jit(solution)/shard_map/ppermute | solution.py:44
  157.4 38.7 %collective-permute-done.4 = bf16[512,512]{1,0:T(8,128)(2,1)S(1)} collective-permute-done((bf16[512,512]{1,0:T(8,128)(2,1)S(1)}, bf16[512,512]{1,0:T(8,128)(2,1)S(1)}, u32[]{:S(2)}, u32[]{:S(2)}) %collective-permute-start.4) | collective-permute-done | bytes 524320 | tf_op jit(solution)/shard_map/ppermute | solution.py:44
  196.1 6.5 %collective-permute-start.5 = (bf16[512,512]{1,0:T(8,128)(2,1)S(1)}, bf16[512,512]{1,0:T(8,128)(2,1)S(1)}, u32[]{:S(2)}, u32[]{:S(2)}) collective-permute-start(bf16[512,512]{1,0:T(8,128)(2,1)S(1)} %collective-permute-done.2.refs_4_.refs_6_.refs_10_.refs_1_), channel_id=1, source_target_pairs={{0,1},{1,2},{2,3},{3,0},{4,5},{5,6},{6,7},{7,4},{8,11},{9,8},{10,9... | collective-permute-start | bytes 1572872 | tf_op jit(solution)/shard_map/ppermute | solution.py:44
  203.1 5.6 %collective-permute-done.5.refs_6_.refs_8_.refs_12_.refs_3_ = bf16[512,512]{1,0:T(8,128)(2,1)S(1)} collective-permute-done((bf16[512,512]{1,0:T(8,128)(2,1)S(1)}, bf16[512,512]{1,0:T(8,128)(2,1)S(1)}, u32[]{:S(2)}, u32[]{:S(2)}) %collective-permute-start.5) | collective-permute-done | bytes 524320 | tf_op jit(solution)/shard_map/ppermute | solution.py:44
  208.7 5.6 %collective-permute-done.6.refs_7_.refs_9_.refs_13_.refs_4_ = bf16[512,512]{1,0:T(8,128)(2,1)S(1)} collective-permute-done((bf16[512,512]{1,0:T(8,128)(2,1)S(1)}, bf16[512,512]{1,0:T(8,128)(2,1)S(1)}, u32[]{:S(2)}, u32[]{:S(2)}) %collective-permute-start.6) | collective-permute-done | bytes 524320 | tf_op jit(solution)/shard_map/ppermute | solution.py:44
  215.7 2.8 collective-permute-start.8
  218.5 7.6 %collective-permute-done.10 = bf16[512,512]{1,0:T(8,128)(2,1)S(1)} collective-permute-done((bf16[512,512]{1,0:T(8,128)(2,1)S(1)}, bf16[512,512]{1,0:T(8,128)(2,1)S(1)}, u32[]{:S(2)}, u32[]{:S(2)}) %collective-permute-start.10) | collective-permute-done | bytes 524320 | tf_op jit(solution)/shard_map/ppermute | solution.py:44
  226.1 1.1 pad_maximum_fusion.refs_3_.refs_5_
  227.2 3.0 collective-permute-done.9.refs_9_.refs_11_.refs_15_.refs_6_
  230.2 3.5 collective-permute-start.13
  233.7 1.9 collective-permute-start.14
  235.9 17.4 %collective-permute-done.14.refs_9_.refs_5_ = bf16[512,512]{1,0:T(8,128)(2,1)} collective-permute-done((bf16[512,512]{1,0:T(8,128)(2,1)S(1)}, bf16[512,512]{1,0:T(8,128)(2,1)}, u32[]{:S(2)}, u32[]{:S(2)}) %collective-permute-start.14) | collective-permute-done | bytes 524320 | tf_op jit(solution)/shard_map/ppermute | solution.py:44
  253.3 2.5 collective-permute-start.17
  256.5 5.2 %project_home.1.refs_3_ = f32[256,640]{1,0:T(8,128)} custom-call(s32[24]{0:T(128)} %pad_add_fusion.refs_0_.table, bf16[256,4096]{1,0:T(8,128)(2,1)} %get-tuple-element.54.refs_1_, bf16[256,4096]{1,0:T(8,128)(2,1)} %copy-done, bf16[512,512]{1,0:T(8,128)(2,1)} %copy-done.1, bf16[512,512]{1,0:T(8,128)(2,1)} %copy-done.3, bf16[512,512]{1,0:T(8,128)(2,1)} %copy-done.5, ...), custom_call_target="tpu_custom_call" | custom-call | flops 1073741824 | bytes 6291456 | tf_op jit(solution)/shard_map/project_home/pallas_call | solution.py:352
  261.9 2.2 collective-permute-done.15.refs_4_
  265.0 6.4 %expand_home.1 = bf16[256,4096]{1,0:T(8,128)(2,1)} custom-call(s32[24]{0:T(128)} %pad_add_fusion.refs_0_.table, bf16[256,4096]{1,0:T(8,128)(2,1)} %get-tuple-element.54.refs_1_, bf16[256,4096]{1,0:T(8,128)(2,1)} %copy-done, f32[256,640]{1,0:T(8,128)} %project_home.1.refs_3_, f32[256,640]{1,0:T(8,128)} %copy-done.24, bf16[512,512]{1,0:T(8,128)(2,1)} %copy-done.1, ...), custom_call_target="tpu_custom_call" | custom-call | flops 1073741824 | bytes 8388608 | tf_op jit(solution)/shard_map/expand_home/pallas_call | solution.py:352
  272.2 1.2 collective-permute-done.18.refs_11_.refs_7_
  274.8 1.1 constant_dynamic-update-slice_fusion
  276.8 2.6 collective-permute-start.20
  279.5 17.9 %collective-permute-done.16 = bf16[256,4096]{1,0:T(8,128)(2,1)S(1)} collective-permute-done((bf16[256,4096]{1,0:T(8,128)(2,1)}, bf16[256,4096]{1,0:T(8,128)(2,1)S(1)}, u32[]{:S(2)}, u32[]{:S(2)}) %collective-permute-start.16) | collective-permute-done | bytes 2097184 | tf_op jit(solution)/shard_map/ppermute | solution.py:44
  297.6 11.5 %collective-permute-done.22 = bf16[512,512]{1,0:T(8,128)(2,1)S(1)} collective-permute-done((bf16[512,512]{1,0:T(8,128)(2,1)S(1)}, bf16[512,512]{1,0:T(8,128)(2,1)S(1)}, u32[]{:S(2)}, u32[]{:S(2)}) %collective-permute-start.22) | collective-permute-done | bytes 524320 | tf_op jit(solution)/shard_map/ppermute | solution.py:44
  309.1 11.5 %collective-permute-start.24 = (bf16[256,4096]{1,0:T(8,128)(2,1)S(1)}, bf16[256,4096]{1,0:T(8,128)(2,1)}, u32[]{:S(2)}, u32[]{:S(2)}) collective-permute-start(bf16[256,4096]{1,0:T(8,128)(2,1)S(1)} %collective-permute-done.16), channel_id=1, source_target_pairs={{0,80},{1,81},{2,82},{3,83},{4,84},{5,85},{6,86},{7,87},{8,56},{9,... | collective-permute-start | bytes 6291464 | tf_op jit(solution)/shard_map/ppermute | solution.py:44
  321.4 2.0 collective-permute-start.25
  323.4 1.7 collective-permute-start.26
  325.1 9.7 %collective-permute-done.28.refs_12_.refs_8_ = bf16[512,512]{1,0:T(8,128)(2,1)S(1)} collective-permute-done((bf16[512,512]{1,0:T(8,128)(2,1)S(1)}, bf16[512,512]{1,0:T(8,128)(2,1)S(1)}, u32[]{:S(2)}, u32[]{:S(2)}) %collective-permute-start.28) | collective-permute-done | bytes 524320 | tf_op jit(solution)/shard_map/ppermute | solution.py:44
  335.4 5.7 %collective-permute-done.26.refs_15_.refs_11_ = bf16[512,512]{1,0:T(8,128)(2,1)S(1)} collective-permute-done((bf16[512,512]{1,0:T(8,128)(2,1)S(1)}, bf16[512,512]{1,0:T(8,128)(2,1)S(1)}, u32[]{:S(2)}, u32[]{:S(2)}) %collective-permute-start.26) | collective-permute-done | bytes 524320 | tf_op jit(solution)/shard_map/ppermute | solution.py:44
  341.1 7.4 %collective-permute-done.29.refs_14_.refs_10_ = bf16[512,512]{1,0:T(8,128)(2,1)S(1)} collective-permute-done((bf16[512,512]{1,0:T(8,128)(2,1)S(1)}, bf16[512,512]{1,0:T(8,128)(2,1)S(1)}, u32[]{:S(2)}, u32[]{:S(2)}) %collective-permute-start.29) | collective-permute-done | bytes 524320 | tf_op jit(solution)/shard_map/ppermute | solution.py:44
  349.3 7.3 %project_first.1.refs_3_ = f32[512,640]{1,0:T(8,128)} custom-call(s32[24]{0:T(128)} %pad_add_fusion.refs_0_.table, bf16[256,4096]{1,0:T(8,128)(2,1)} %collective-permute-done.24.refs_1_, bf16[256,4096]{1,0:T(8,128)(2,1)} %collective-permute-done.19.refs_2_, bf16[1024,512]{1,0:T(8,128)(2,1)} %pad_maximum_fusion.refs_3_.refs_5_, ...), custom_call_target="tpu_custom_call" | custom-call | flops 2147483648 | bytes 8388608 | tf_op jit(solution)/shard_map/project_first/pallas_call | solution.py:352
  356.7 17.2 %collective-permute-start.30 = (f32[512,640]{1,0:T(8,128)}, f32[512,640]{1,0:T(8,128)}, u32[]{:S(2)}, u32[]{:S(2)}) collective-permute-start(f32[512,640]{1,0:T(8,128)} %project_first.1.refs_3_), channel_id=1, source_target_pairs={{0,8},{1,9},{2,10},{3,11},{4,12},{5,13},{6,14},{7,15},{8,0},{9,1},... | collective-permute-start | bytes 3932168 | tf_op jit(solution)/shard_map/ppermute | solution.py:44
  374.8 12.5 %collective-permute-done.31.refs_16_.refs_12_ = bf16[512,512]{1,0:T(8,128)(2,1)S(1)} collective-permute-done((bf16[512,512]{1,0:T(8,128)(2,1)S(1)}, bf16[512,512]{1,0:T(8,128)(2,1)S(1)}, u32[]{:S(2)}, u32[]{:S(2)}) %collective-permute-start.31) | collective-permute-done | bytes 524320 | tf_op jit(solution)/shard_map/ppermute | solution.py:44
  388.1 11.9 %first_second.1 = (bf16[256,4096]{1,0:T(8,128)(2,1)}, bf16[256,4096]{1,0:T(8,128)(2,1)}, f32[512,640]{1,0:T(8,128)}) custom-call(s32[24]{0:T(128)} %pad_add_fusion.refs_0_.table, bf16[256,4096]{1,0:T(8,128)(2,1)} %collective-permute-done.24.refs_1_, bf16[256,4096]{1,0:T(8,128)(2,1)} %collective-permute-done.19.refs_2_, f32[512,640]{1,0:T(8,128)} %project_first.1.refs_3_, ...), custom_call_target="tpu_custom_call" | custom-call | flops 4294967296 | bytes 16777216 | tf_op jit(solution)/shard_map/first_second/pallas_call | solution.py:352
  401.0 9.2 %collective-permute-start.34 = (bf16[1024,512]{1,0:T(8,128)(2,1)S(1)}, bf16[1024,512]{1,0:T(8,128)(2,1)S(1)}, u32[]{:S(2)}, u32[]{:S(2)}) collective-permute-start(bf16[1024,512]{1,0:T(8,128)(2,1)S(1)} %collective-permute-done.33.refs_15_.refs_7_), channel_id=1, source_target_pairs={{0,1},{1,2},{2,3},{3,0},{4,5},{5,6},{6,7},{7,4},{8,11},{9,8},{10,9... | collective-permute-start | bytes 3145736 | tf_op jit(solution)/shard_map/ppermute | solution.py:44
  411.3 11.7 %second_third.1 = (bf16[256,4096]{1,0:T(8,128)(2,1)}, bf16[256,4096]{1,0:T(8,128)(2,1)}, f32[512,640]{1,0:T(8,128)}) custom-call(s32[24]{0:T(128)} %pad_add_fusion.refs_0_.table, bf16[256,4096]{1,0:T(8,128)(2,1)} %get-tuple-element.88.refs_1_, bf16[256,4096]{1,0:T(8,128)(2,1)} %get-tuple-element.89.refs_2_, f32[512,640]{1,0:T(8,128)} %get-tuple-element.90.refs_3_, ...), custom_call_target="tpu_custom_call" | custom-call | flops 3758096384 | bytes 15728640 | tf_op jit(solution)/shard_map/second_third/pallas_call | solution.py:352
  424.9 4.7 %third_rest.1.refs_3_ = f32[512,640]{1,0:T(8,128)} custom-call(s32[24]{0:T(128)} %pad_add_fusion.refs_0_.table, bf16[256,4096]{1,0:T(8,128)(2,1)} %get-tuple-element.92.refs_1_, bf16[256,4096]{1,0:T(8,128)(2,1)} %get-tuple-element.93.refs_2_, f32[512,640]{1,0:T(8,128)} %get-tuple-element.94.refs_3_, bf16[1024,512]{1,0:T(8,128)(2,1)} %copy-done.16), custom_call_target="tpu_custom_call" | custom-call | flops 536870912 | bytes 5242880 | tf_op jit(solution)/shard_map/third_rest/pallas_call | solution.py:352
  429.6 2.5 collective-permute-start.35
  432.1 2.9 collective-permute-done.35.refs_4_
  435.0 1.1 copy-done.21
  436.0 10.6 %third_home.1 = (bf16[256,4096]{1,0:T(8,128)(2,1)}, bf16[256,4096]{1,0:T(8,128)(2,1)}, f32[256,640]{1,0:T(8,128)}) custom-call(s32[24]{0:T(128)} %pad_add_fusion.refs_0_.table, bf16[256,4096]{1,0:T(8,128)(2,1)} %get-tuple-element.92.refs_1_, bf16[256,4096]{1,0:T(8,128)(2,1)} %get-tuple-element.93.refs_2_, f32[512,640]{1,0:T(8,128)} %third_rest.1.refs_3_, ...), custom_call_target="tpu_custom_call" | custom-call | flops 3221225472 | bytes 16777216 | tf_op jit(solution)/shard_map/third_home/pallas_call | solution.py:352
  447.2 4.8 %collective-permute-done.37.theirs = f32[256,640]{1,0:T(8,128)S(1)} collective-permute-done((f32[256,640]{1,0:T(8,128)}, f32[256,640]{1,0:T(8,128)S(1)}, u32[]{:S(2)}, u32[]{:S(2)}) %collective-permute-start.37) | collective-permute-done | bytes 655392 | tf_op jit(solution)/shard_map/ppermute | solution.py:44
  453.7 9.0 %final_layer.1 = bf16[256,8192]{1,0:T(8,128)(2,1)} custom-call(s32[24]{0:T(128)} %pad_add_fusion.refs_0_.table, bf16[256,4096]{1,0:T(8,128)(2,1)} %get-tuple-element.95.keep, bf16[256,4096]{1,0:T(8,128)(2,1)} %copy-done.20, f32[256,640]{1,0:T(8,128)} %get-tuple-element.97.mine, f32[256,640]{1,0:T(8,128)} %copy-done.25, bf16[512,512]{1,0:T(8,128)(2,1)} %copy-done.1, ...), custom_call_target="tpu_custom_call" | custom-call | flops 2147483648 | bytes 16777216 | tf_op jit(solution)/shard_map/final_layer/pallas_call | solution.py:423
  (131 shorter events, 17.9 us)
Async XLA Ops:
  131.7 3.2 collective-permute-start
  134.9 4.4 collective-permute-start.1
  141.9 88.2 %collective-permute-start.11 = (bf16[256,4096]{1,0:T(8,128)(2,1)S(1)}, bf16[256,4096]{1,0:T(8,128)(2,1)}, u32[]{:S(2)}, u32[]{:S(2)}) collective-permute-start(bf16[256,4096]{1,0:T(8,128)(2,1)S(1)} %broadcast_select_fusion), channel_id=1, source_target_pairs={{0,16},{1,17},{2,18},{3,19},{4,20},{5,21},{6,22},{7,23},{8,56},{9,... | collective-permute-start | bytes 6291464 | tf_op jit(solution)/shard_map/ppermute | solution.py:44
  144.9 111.6 %copy-start.1 = (bf16[512,512]{1,0:T(8,128)(2,1)}, bf16[512,512]{1,0:T(8,128)(2,1)S(1)}, u32[]{:S(2)}) copy-start(bf16[512,512]{1,0:T(8,128)(2,1)S(1)} %get-tuple-element.78.refs_3_.refs_5_.refs_9_.refs_0_) | copy-start | bytes 1572868
  144.9 12.5 %collective-permute-start.2 = (bf16[512,512]{1,0:T(8,128)(2,1)S(1)}, bf16[512,512]{1,0:T(8,128)(2,1)S(1)}, u32[]{:S(2)}, u32[]{:S(2)}) collective-permute-start(bf16[512,512]{1,0:T(8,128)(2,1)S(1)} %get-tuple-element.78.refs_3_.refs_5_.refs_9_.refs_0_), channel_id=1, source_target_pairs={{0,4},{1,5},{2,6},{3,7},{4,0},{5,1},{6,2},{7,3},{8,12},{9,13},{10,... | collective-permute-start | bytes 1572872 | tf_op jit(solution)/shard_map/ppermute | solution.py:44
  146.2 11.2 %collective-permute-start.3 = (bf16[512,512]{1,0:T(8,128)(2,1)S(1)}, bf16[512,512]{1,0:T(8,128)(2,1)S(1)}, u32[]{:S(2)}, u32[]{:S(2)}) collective-permute-start(bf16[512,512]{1,0:T(8,128)(2,1)S(1)} %get-tuple-element.78.refs_3_.refs_5_.refs_9_.refs_0_), channel_id=1, source_target_pairs={{0,1},{1,2},{2,3},{3,0},{4,5},{5,6},{6,7},{7,4},{8,11},{9,8},{10,9... | collective-permute-start | bytes 1572872 | tf_op jit(solution)/shard_map/ppermute | solution.py:44
  150.0 46.2 %collective-permute-start.4 = (bf16[512,512]{1,0:T(8,128)(2,1)S(1)}, bf16[512,512]{1,0:T(8,128)(2,1)S(1)}, u32[]{:S(2)}, u32[]{:S(2)}) collective-permute-start(bf16[512,512]{1,0:T(8,128)(2,1)S(1)} %get-tuple-element.98), channel_id=1, source_target_pairs={{0,16},{1,17},{2,18},{3,19},{4,20},{5,21},{6,22},{7,23},{8,24},{9,... | collective-permute-start | bytes 1572872 | tf_op jit(solution)/shard_map/ppermute | solution.py:44
  157.4 99.1 %copy-start.3 = (bf16[512,512]{1,0:T(8,128)(2,1)}, bf16[512,512]{1,0:T(8,128)(2,1)S(1)}, u32[]{:S(2)}) copy-start(bf16[512,512]{1,0:T(8,128)(2,1)S(1)} %collective-permute-done.2.refs_4_.refs_6_.refs_10_.refs_1_) | copy-start | bytes 1572868
  157.4 99.1 %copy-start.5 = (bf16[512,512]{1,0:T(8,128)(2,1)}, bf16[512,512]{1,0:T(8,128)(2,1)S(1)}, u32[]{:S(2)}) copy-start(bf16[512,512]{1,0:T(8,128)(2,1)S(1)} %collective-permute-done.3.refs_5_.refs_7_.refs_11_.refs_2_) | copy-start | bytes 1572868
  196.1 12.6 %collective-permute-start.5 = (bf16[512,512]{1,0:T(8,128)(2,1)S(1)}, bf16[512,512]{1,0:T(8,128)(2,1)S(1)}, u32[]{:S(2)}, u32[]{:S(2)}) collective-permute-start(bf16[512,512]{1,0:T(8,128)(2,1)S(1)} %collective-permute-done.2.refs_4_.refs_6_.refs_10_.refs_1_), channel_id=1, source_target_pairs={{0,1},{1,2},{2,3},{3,0},{4,5},{5,6},{6,7},{7,4},{8,11},{9,8},{10,9... | collective-permute-start | bytes 1572872 | tf_op jit(solution)/shard_map/ppermute | solution.py:44
  202.6 11.7 %collective-permute-start.6 = (bf16[512,512]{1,0:T(8,128)(2,1)S(1)}, bf16[512,512]{1,0:T(8,128)(2,1)S(1)}, u32[]{:S(2)}, u32[]{:S(2)}) collective-permute-start(bf16[512,512]{1,0:T(8,128)(2,1)S(1)} %collective-permute-done.3.refs_5_.refs_7_.refs_11_.refs_2_), channel_id=1, source_target_pairs={{0,1},{1,2},{2,3},{3,0},{4,5},{5,6},{6,7},{7,4},{8,11},{9,8},{10,9... | collective-permute-start | bytes 1572872 | tf_op jit(solution)/shard_map/ppermute | solution.py:44
  203.1 11.6 %collective-permute-start.7 = (bf16[512,512]{1,0:T(8,128)(2,1)S(1)}, bf16[512,512]{1,0:T(8,128)(2,1)S(1)}, u32[]{:S(2)}, u32[]{:S(2)}) collective-permute-start(bf16[512,512]{1,0:T(8,128)(2,1)S(1)} %collective-permute-done.4), channel_id=1, source_target_pairs={{0,16},{1,17},{2,18},{3,19},{4,20},{5,21},{6,22},{7,23},{8,24},{9,... | collective-permute-start | bytes 1572872 | tf_op jit(solution)/shard_map/ppermute | solution.py:44
  208.7 47.8 %copy-start.7 = (bf16[512,512]{1,0:T(8,128)(2,1)}, bf16[512,512]{1,0:T(8,128)(2,1)S(1)}, u32[]{:S(2)}) copy-start(bf16[512,512]{1,0:T(8,128)(2,1)S(1)} %collective-permute-done.5.refs_6_.refs_8_.refs_12_.refs_3_) | copy-start | bytes 1572868
  214.4 42.2 %copy-start.9 = (bf16[512,512]{1,0:T(8,128)(2,1)}, bf16[512,512]{1,0:T(8,128)(2,1)S(1)}, u32[]{:S(2)}) copy-start(bf16[512,512]{1,0:T(8,128)(2,1)S(1)} %collective-permute-done.6.refs_7_.refs_9_.refs_13_.refs_4_) | copy-start | bytes 1572868
  214.8 11.3 %collective-permute-start.10 = (bf16[512,512]{1,0:T(8,128)(2,1)S(1)}, bf16[512,512]{1,0:T(8,128)(2,1)S(1)}, u32[]{:S(2)}, u32[]{:S(2)}) collective-permute-start(bf16[512,512]{1,0:T(8,128)(2,1)S(1)} %collective-permute-done.7), channel_id=1, source_target_pairs={{0,4},{1,5},{2,6},{3,7},{4,0},{5,1},{6,2},{7,3},{8,12},{9,13},{10,... | collective-permute-start | bytes 1572872 | tf_op jit(solution)/shard_map/ppermute | solution.py:44
  215.7 11.5 %collective-permute-start.8 = (bf16[512,512]{1,0:T(8,128)(2,1)S(1)}, bf16[512,512]{1,0:T(8,128)(2,1)S(1)}, u32[]{:S(2)}, u32[]{:S(2)}) collective-permute-start(bf16[512,512]{1,0:T(8,128)(2,1)S(1)} %collective-permute-done.5.refs_6_.refs_8_.refs_12_.refs_3_), channel_id=1, source_target_pairs={{0,1},{1,2},{2,3},{3,0},{4,5},{5,6},{6,7},{7,4},{8,11},{9,8},{10,9... | collective-permute-start | bytes 1572872 | tf_op jit(solution)/shard_map/ppermute | solution.py:44
  218.4 11.7 %collective-permute-start.9 = (bf16[512,512]{1,0:T(8,128)(2,1)S(1)}, bf16[512,512]{1,0:T(8,128)(2,1)S(1)}, u32[]{:S(2)}, u32[]{:S(2)}) collective-permute-start(bf16[512,512]{1,0:T(8,128)(2,1)S(1)} %collective-permute-done.6.refs_7_.refs_9_.refs_13_.refs_4_), channel_id=1, source_target_pairs={{0,1},{1,2},{2,3},{3,0},{4,5},{5,6},{6,7},{7,4},{8,11},{9,8},{10,9... | collective-permute-start | bytes 1572872 | tf_op jit(solution)/shard_map/ppermute | solution.py:44
  227.2 29.3 %copy-start.11 = (bf16[512,512]{1,0:T(8,128)(2,1)}, bf16[512,512]{1,0:T(8,128)(2,1)S(1)}, u32[]{:S(2)}) copy-start(bf16[512,512]{1,0:T(8,128)(2,1)S(1)} %collective-permute-done.8.refs_8_.refs_10_.refs_14_.refs_5_) | copy-start | bytes 1572868
  230.2 23.1 %collective-permute-start.13 = (bf16[1024,512]{1,0:T(8,128)(2,1)}, bf16[1024,512]{1,0:T(8,128)(2,1)}, u32[]{:S(2)}, u32[]{:S(2)}) collective-permute-start(bf16[1024,512]{1,0:T(8,128)(2,1)} %pad_maximum_fusion.refs_3_.refs_5_), channel_id=1, source_target_pairs={{0,1},{1,2},{2,3},{3,0},{4,5},{5,6},{6,7},{7,4},{8,11},{9,8},{10,9... | collective-permute-start | bytes 3145736 | tf_op jit(solution)/shard_map/ppermute | solution.py:44
  233.7 39.7 %collective-permute-start.19 = (bf16[256,4096]{1,0:T(8,128)(2,1)}, bf16[256,4096]{1,0:T(8,128)(2,1)}, u32[]{:S(2)}, u32[]{:S(2)}) collective-permute-start(bf16[256,4096]{1,0:T(8,128)(2,1)} %collective-permute-done.11), channel_id=1, source_target_pairs={{0,80},{1,81},{2,82},{3,83},{4,84},{5,85},{6,86},{7,87},{8,56},{9,... | collective-permute-start | bytes 6291464 | tf_op jit(solution)/shard_map/ppermute | solution.py:44
  233.7 19.6 %collective-permute-start.14 = (bf16[512,512]{1,0:T(8,128)(2,1)S(1)}, bf16[512,512]{1,0:T(8,128)(2,1)}, u32[]{:S(2)}, u32[]{:S(2)}) collective-permute-start(bf16[512,512]{1,0:T(8,128)(2,1)S(1)} %get-tuple-element.78.refs_3_.refs_5_.refs_9_.refs_0_), channel_id=1, source_target_pairs={{0,16},{1,17},{2,18},{3,19},{4,20},{5,21},{6,22},{7,23},{8,24},{9,... | collective-permute-start | bytes 1572872 | tf_op jit(solution)/shard_map/ppermute | solution.py:44
  235.6 17.6 %collective-permute-start.12 = (bf16[512,512]{1,0:T(8,128)(2,1)S(1)}, bf16[512,512]{1,0:T(8,128)(2,1)}, u32[]{:S(2)}, u32[]{:S(2)}) collective-permute-start(bf16[512,512]{1,0:T(8,128)(2,1)S(1)} %collective-permute-done.8.refs_8_.refs_10_.refs_14_.refs_5_), channel_id=1, source_target_pairs={{0,1},{1,2},{2,3},{3,0},{4,5},{5,6},{6,7},{7,4},{8,11},{9,8},{10,9... | collective-permute-start | bytes 1572872 | tf_op jit(solution)/shard_map/ppermute | solution.py:44
  253.3 20.1 %collective-permute-start.17 = (bf16[1024,512]{1,0:T(8,128)(2,1)}, bf16[1024,512]{1,0:T(8,128)(2,1)}, u32[]{:S(2)}, u32[]{:S(2)}) collective-permute-start(bf16[1024,512]{1,0:T(8,128)(2,1)} %collective-permute-done.13.refs_4_.refs_6_), channel_id=1, source_target_pairs={{0,1},{1,2},{2,3},{3,0},{4,5},{5,6},{6,7},{7,4},{8,11},{9,8},{10,9... | collective-permute-start | bytes 3145736 | tf_op jit(solution)/shard_map/ppermute | solution.py:44
  261.7 2.4 collective-permute-start.15
  261.8 11.6 %collective-permute-start.18 = (bf16[512,512]{1,0:T(8,128)(2,1)}, bf16[512,512]{1,0:T(8,128)(2,1)S(1)}, u32[]{:S(2)}, u32[]{:S(2)}) collective-permute-start(bf16[512,512]{1,0:T(8,128)(2,1)} %collective-permute-done.14.refs_9_.refs_5_), channel_id=1, source_target_pairs={{0,1},{1,2},{2,3},{3,0},{4,5},{5,6},{6,7},{7,4},{8,11},{9,8},{10,9... | collective-permute-start | bytes 1572872 | tf_op jit(solution)/shard_map/ppermute | solution.py:44
  271.4 26.0 %collective-permute-start.16 = (bf16[256,4096]{1,0:T(8,128)(2,1)}, bf16[256,4096]{1,0:T(8,128)(2,1)S(1)}, u32[]{:S(2)}, u32[]{:S(2)}) collective-permute-start(bf16[256,4096]{1,0:T(8,128)(2,1)} %expand_home.1), channel_id=1, source_target_pairs={{0,16},{1,17},{2,18},{3,19},{4,20},{5,21},{6,22},{7,23},{8,56},{9,... | collective-permute-start | bytes 6291464 | tf_op jit(solution)/shard_map/ppermute | solution.py:44
  273.4 47.2 %copy-start.26 = (bf16[512,512]{1,0:T(8,128)(2,1)}, bf16[512,512]{1,0:T(8,128)(2,1)S(1)}, u32[]{:S(2)}) copy-start(bf16[512,512]{1,0:T(8,128)(2,1)S(1)} %collective-permute-done.18.refs_11_.refs_7_) | copy-start | bytes 1572868
  275.9 72.6 %collective-permute-start.27 = (bf16[4096,512]{1,0:T(8,128)(2,1)S(1)}, bf16[4096,512]{1,0:T(8,128)(2,1)S(1)}, u32[]{:S(2)}, u32[]{:S(2)}) collective-permute-start(bf16[4096,512]{1,0:T(8,128)(2,1)S(1)} %constant_dynamic-update-slice_fusion), channel_id=1, source_target_pairs={{0,8},{1,9},{2,10},{3,11},{4,12},{5,13},{6,14},{7,15},{8,0},{9,1},... | collective-permute-start | bytes 12582920 | tf_op jit(solution)/shard_map/ppermute | solution.py:44
  276.8 20.8 %collective-permute-start.20 = (bf16[1024,512]{1,0:T(8,128)(2,1)}, bf16[1024,512]{1,0:T(8,128)(2,1)S(1)}, u32[]{:S(2)}, u32[]{:S(2)}) collective-permute-start(bf16[1024,512]{1,0:T(8,128)(2,1)} %collective-permute-done.17.refs_5_.refs_7_), channel_id=1, source_target_pairs={{0,1},{1,2},{2,3},{3,0},{4,5},{5,6},{6,7},{7,4},{8,11},{9,8},{10,9... | collective-permute-start | bytes 3145736 | tf_op jit(solution)/shard_map/ppermute | solution.py:44
  279.3 18.2 %collective-permute-start.23 = (bf16[512,512]{1,0:T(8,128)(2,1)}, bf16[512,512]{1,0:T(8,128)(2,1)S(1)}, u32[]{:S(2)}, u32[]{:S(2)}) collective-permute-start(bf16[512,512]{1,0:T(8,128)(2,1)} %collective-permute-done.14.refs_9_.refs_5_), channel_id=1, source_target_pairs={{0,4},{1,5},{2,6},{3,7},{4,0},{5,1},{6,2},{7,3},{8,12},{9,13},{10,... | collective-permute-start | bytes 1572872 | tf_op jit(solution)/shard_map/ppermute | solution.py:44
  279.4 18.1 %collective-permute-start.21 = (bf16[512,512]{1,0:T(8,128)(2,1)S(1)}, bf16[512,512]{1,0:T(8,128)(2,1)S(1)}, u32[]{:S(2)}, u32[]{:S(2)}) collective-permute-start(bf16[512,512]{1,0:T(8,128)(2,1)S(1)} %collective-permute-done.18.refs_11_.refs_7_), channel_id=1, source_target_pairs={{0,1},{1,2},{2,3},{3,0},{4,5},{5,6},{6,7},{7,4},{8,11},{9,8},{10,9... | collective-permute-start | bytes 1572872 | tf_op jit(solution)/shard_map/ppermute | solution.py:44
  297.4 11.7 %collective-permute-start.22 = (bf16[512,512]{1,0:T(8,128)(2,1)S(1)}, bf16[512,512]{1,0:T(8,128)(2,1)S(1)}, u32[]{:S(2)}, u32[]{:S(2)}) collective-permute-start(bf16[512,512]{1,0:T(8,128)(2,1)S(1)} %copy-done.36), channel_id=1, source_target_pairs={{0,4},{1,5},{2,6},{3,7},{4,0},{5,1},{6,2},{7,3},{8,12},{9,13},{10,... | collective-permute-start | bytes 1572872 | tf_op jit(solution)/shard_map/ppermute | solution.py:44
  297.6 50.9 %copy-start.28 = (bf16[512,512]{1,0:T(8,128)(2,1)}, bf16[512,512]{1,0:T(8,128)(2,1)S(1)}, u32[]{:S(2)}) copy-start(bf16[512,512]{1,0:T(8,128)(2,1)S(1)} %collective-permute-done.21.refs_13_.refs_9_) | copy-start | bytes 1572868
  297.6 51.7 %copy-start.23 = (bf16[1024,512]{1,0:T(8,128)(2,1)}, bf16[1024,512]{1,0:T(8,128)(2,1)S(1)}, u32[]{:S(2)}) copy-start(bf16[1024,512]{1,0:T(8,128)(2,1)S(1)} %collective-permute-done.20.refs_6_.refs_8_) | copy-start | bytes 3145732
  309.1 40.1 %collective-permute-start.24 = (bf16[256,4096]{1,0:T(8,128)(2,1)S(1)}, bf16[256,4096]{1,0:T(8,128)(2,1)}, u32[]{:S(2)}, u32[]{:S(2)}) collective-permute-start(bf16[256,4096]{1,0:T(8,128)(2,1)S(1)} %collective-permute-done.16), channel_id=1, source_target_pairs={{0,80},{1,81},{2,82},{3,83},{4,84},{5,85},{6,86},{7,87},{8,56},{9,... | collective-permute-start | bytes 6291464 | tf_op jit(solution)/shard_map/ppermute | solution.py:44
  320.6 14.1 %collective-permute-start.28 = (bf16[512,512]{1,0:T(8,128)(2,1)S(1)}, bf16[512,512]{1,0:T(8,128)(2,1)S(1)}, u32[]{:S(2)}, u32[]{:S(2)}) collective-permute-start(bf16[512,512]{1,0:T(8,128)(2,1)S(1)} %collective-permute-done.18.refs_11_.refs_7_), channel_id=1, source_target_pairs={{0,4},{1,5},{2,6},{3,7},{4,0},{5,1},{6,2},{7,3},{8,12},{9,13},{10,... | collective-permute-start | bytes 1572872 | tf_op jit(solution)/shard_map/ppermute | solution.py:44
  321.4 35.3 %copy-start.15 = (bf16[1024,512]{1,0:T(8,128)(2,1)}, bf16[1024,512]{1,0:T(8,128)(2,1)S(1)}, u32[]{:S(2)}) copy-start(bf16[1024,512]{1,0:T(8,128)(2,1)S(1)} %pad_maximum_fusion.1.refs_13_.refs_5_) | copy-start | bytes 3145732
  321.4 27.1 %collective-permute-start.25 = (bf16[1024,512]{1,0:T(8,128)(2,1)S(1)}, bf16[1024,512]{1,0:T(8,128)(2,1)S(1)}, u32[]{:S(2)}, u32[]{:S(2)}) collective-permute-start(bf16[1024,512]{1,0:T(8,128)(2,1)S(1)} %pad_maximum_fusion.1.refs_13_.refs_5_), channel_id=1, source_target_pairs={{0,1},{1,2},{2,3},{3,0},{4,5},{5,6},{6,7},{7,4},{8,11},{9,8},{10,9... | collective-permute-start | bytes 3145736 | tf_op jit(solution)/shard_map/ppermute | solution.py:44
  323.4 17.7 %collective-permute-start.26 = (bf16[512,512]{1,0:T(8,128)(2,1)S(1)}, bf16[512,512]{1,0:T(8,128)(2,1)S(1)}, u32[]{:S(2)}, u32[]{:S(2)}) collective-permute-start(bf16[512,512]{1,0:T(8,128)(2,1)S(1)} %collective-permute-done.21.refs_13_.refs_9_), channel_id=1, source_target_pairs={{0,1},{1,2},{2,3},{3,0},{4,5},{5,6},{6,7},{7,4},{8,11},{9,8},{10,9... | collective-permute-start | bytes 1572872 | tf_op jit(solution)/shard_map/ppermute | solution.py:44
  334.7 13.7 %collective-permute-start.29 = (bf16[512,512]{1,0:T(8,128)(2,1)S(1)}, bf16[512,512]{1,0:T(8,128)(2,1)S(1)}, u32[]{:S(2)}, u32[]{:S(2)}) collective-permute-start(bf16[512,512]{1,0:T(8,128)(2,1)S(1)} %collective-permute-done.21.refs_13_.refs_9_), channel_id=1, source_target_pairs={{0,4},{1,5},{2,6},{3,7},{4,0},{5,1},{6,2},{7,3},{8,12},{9,13},{10,... | collective-permute-start | bytes 1572872 | tf_op jit(solution)/shard_map/ppermute | solution.py:44
  356.7 30.7 %collective-permute-start.30 = (f32[512,640]{1,0:T(8,128)}, f32[512,640]{1,0:T(8,128)}, u32[]{:S(2)}, u32[]{:S(2)}) collective-permute-start(f32[512,640]{1,0:T(8,128)} %project_first.1.refs_3_), channel_id=1, source_target_pairs={{0,8},{1,9},{2,10},{3,11},{4,12},{5,13},{6,14},{7,15},{8,0},{9,1},... | collective-permute-start | bytes 3932168 | tf_op jit(solution)/shard_map/ppermute | solution.py:44
  373.8 13.5 %collective-permute-start.31 = (bf16[512,512]{1,0:T(8,128)(2,1)S(1)}, bf16[512,512]{1,0:T(8,128)(2,1)S(1)}, u32[]{:S(2)}, u32[]{:S(2)}) collective-permute-start(bf16[512,512]{1,0:T(8,128)(2,1)S(1)} %copy-done.31), channel_id=1, source_target_pairs={{0,4},{1,5},{2,6},{3,7},{4,0},{5,1},{6,2},{7,3},{8,12},{9,13},{10,... | collective-permute-start | bytes 1572872 | tf_op jit(solution)/shard_map/ppermute | solution.py:44
  374.8 26.3 %collective-permute-start.33 = (bf16[1024,512]{1,0:T(8,128)(2,1)S(1)}, bf16[1024,512]{1,0:T(8,128)(2,1)S(1)}, u32[]{:S(2)}, u32[]{:S(2)}) collective-permute-start(bf16[1024,512]{1,0:T(8,128)(2,1)S(1)} %collective-permute-done.25.refs_14_.refs_6_), channel_id=1, source_target_pairs={{0,1},{1,2},{2,3},{3,0},{4,5},{5,6},{6,7},{7,4},{8,11},{9,8},{10,9... | collective-permute-start | bytes 3145736 | tf_op jit(solution)/shard_map/ppermute | solution.py:44
  400.0 10.2 %collective-permute-start.32 = (f32[512,640]{1,0:T(8,128)}, f32[512,640]{1,0:T(8,128)S(1)}, u32[]{:S(2)}, u32[]{:S(2)}) collective-permute-start(f32[512,640]{1,0:T(8,128)} %get-tuple-element.90.refs_3_), channel_id=1, source_target_pairs={{0,8},{1,9},{2,10},{3,11},{4,12},{5,13},{6,14},{7,15},{8,0},{9,1},... | collective-permute-start | bytes 3932168 | tf_op jit(solution)/shard_map/ppermute | solution.py:44
  401.0 22.9 %collective-permute-start.34 = (bf16[1024,512]{1,0:T(8,128)(2,1)S(1)}, bf16[1024,512]{1,0:T(8,128)(2,1)S(1)}, u32[]{:S(2)}, u32[]{:S(2)}) collective-permute-start(bf16[1024,512]{1,0:T(8,128)(2,1)S(1)} %collective-permute-done.33.refs_15_.refs_7_), channel_id=1, source_target_pairs={{0,1},{1,2},{2,3},{3,0},{4,5},{5,6},{6,7},{7,4},{8,11},{9,8},{10,9... | collective-permute-start | bytes 3145736 | tf_op jit(solution)/shard_map/ppermute | solution.py:44
  429.6 5.4 %collective-permute-start.35 = (f32[512,640]{1,0:T(8,128)}, f32[512,640]{1,0:T(8,128)S(1)}, u32[]{:S(2)}, u32[]{:S(2)}) collective-permute-start(f32[512,640]{1,0:T(8,128)} %third_rest.1.refs_3_), channel_id=1, source_target_pairs={{0,8},{1,9},{2,10},{3,11},{4,12},{5,13},{6,14},{7,15},{8,0},{9,1},... | collective-permute-start | bytes 3932168 | tf_op jit(solution)/shard_map/ppermute | solution.py:44
  446.6 5.4 %collective-permute-start.36 = (bf16[256,4096]{1,0:T(8,128)(2,1)}, bf16[256,4096]{1,0:T(8,128)(2,1)S(1)}, u32[]{:S(2)}, u32[]{:S(2)}) collective-permute-start(bf16[256,4096]{1,0:T(8,128)(2,1)} %get-tuple-element.96), channel_id=1, source_target_pairs={{0,8},{1,9},{2,10},{3,11},{4,12},{5,13},{6,14},{7,15},{8,0},{9,1},... | collective-permute-start | bytes 6291464 | tf_op jit(solution)/shard_map/ppermute | solution.py:44
  447.1 4.9 %collective-permute-start.37 = (f32[256,640]{1,0:T(8,128)}, f32[256,640]{1,0:T(8,128)S(1)}, u32[]{:S(2)}, u32[]{:S(2)}) collective-permute-start(f32[256,640]{1,0:T(8,128)} %get-tuple-element.97.mine), channel_id=1, source_target_pairs={{0,8},{1,9},{2,10},{3,11},{4,12},{5,13},{6,14},{7,15},{8,0},{9,1},... | collective-permute-start | bytes 1966088 | tf_op jit(solution)/shard_map/ppermute | solution.py:44
  (27 other events, 207.8 us)
where the time goes:
time: 467 us; the launch traced here: 463 us
  Pallas kernels  198 us (42%)
  waiting for transfers between devices  168 us (36%)
  starting transfers between devices  81.1 us (17%)
  local copies, waits for them, and re-layouts  9.87 us (2%)
    ppermute x38, waiting for transfers between devices, shift(): return lax.ppermute(value, AXES, pairs)  168 us
    pallas_call x1, Pallas kernels, update_call(): pl.pallas_call(update_kernel, grid_spec=pltpu.PrefetchScalarGridSpec(num_...  131 us
    ppermute x38, starting transfers between devices, shift(): return lax.ppermute(value, AXES, pairs)  81.1 us
    pallas_call x7, Pallas kernels, layer_call(): pl.pallas_call(functools.partial(layer_kernel, plan), in_specs=[pl.BlockS...  57.8 us
  transfers between devices with their start and end apart: 38, of which 21 were waited for; matrix products, arithmetic and copies ran while one was open for 1% of the time, Pallas kernels for 8%

commit v1 on v0

--- a/solution.py
+++ b/solution.py
@@ -25,8 +25,9 @@
 HALF = D // 2
 LANES = 128
 VMEM = 56 * 1024 * 1024
-UPDATE_STEPS = 4
+UPDATE_STEPS = 8
 SUB_STEP = SUB // UPDATE_STEPS
+COST = pl.CostEstimate(flops=1, bytes_accessed=1, transcendentals=0)
 AHEAD = 3
 
 
@@ -58,17 +59,6 @@
 
 def to_chip(value, steps):
     return shift(value, lambda chip, core, xlo, z: (chip + steps, core, xlo, z))
-
-
-def to_next(value, hop):
-    def move(chip, core, xlo, z):
-        xhi, y = divmod(chip, 4)
-        start = (y - hop + 2 * hop * core) % 4
-        if start >= 2 and hop == ((start + core) % 2):
-            xhi = 1 - xhi
-        return xhi * 4 + (y + 1 - 2 * core) % 4, core, xlo, z
-
-    return shift(value, move)
 
 
 def adamw_update(master, moment, second, gradient):
@@ -87,7 +77,7 @@
     moment_ref,
     second_ref,
     gradient_ref,
-    whole,
+    whole_ref,
     master_out,
     moment_out,
     second_out,
@@ -95,26 +85,8 @@
     give_rows,
     keep,
     give,
-    sems,
 ):
-    step = pl.program_id(0)
-    core = core_ref[0]
-
-    def copies():
-        for part in range(8):
-            for side, target in ((core, keep), (1 - core, give)):
-                column = pl.multiple_of(part * 2 * SUB + side * SUB, SUB)
-                yield pltpu.make_async_copy(
-                    whole.at[:, pl.ds(column, SUB)],
-                    target.at[:, pl.ds(part * SUB, SUB)],
-                    sems.at[part, 0 if target is keep else 1],
-                )
-
-    @pl.when(step == 0)
-    def _():
-        for copy in copies():
-            copy.start()
-
+    lower = core_ref[0] == 0
     new_master, new_moment, new_second = adamw_update(
         master_ref[...], moment_ref[...], second_ref[...], gradient_ref[...]
     )
@@ -123,34 +95,34 @@
     second_out[...] = new_second
     first = new_master[0].astype(jnp.bfloat16)
     last = new_master[1].astype(jnp.bfloat16)
-    keep_rows[...] = jnp.where(core == 0, first, last)
-    give_rows[...] = jnp.where(core == 0, last, first)
-
-    @pl.when(step == UPDATE_STEPS - 1)
-    def _():
-        for copy in copies():
-            copy.wait()
+    keep_rows[...] = jnp.where(lower, first, last)
+    give_rows[...] = jnp.where(lower, last, first)
+    for part in range(8 // UPDATE_STEPS):
+        first = whole_ref[:, 2 * part * SUB : (2 * part + 1) * SUB]
+        last = whole_ref[:, (2 * part + 1) * SUB : (2 * part + 2) * SUB]
+        keep[:, part * SUB : (part + 1) * SUB] = jnp.where(lower, first, last)
+        give[:, part * SUB : (part + 1) * SUB] = jnp.where(lower, last, first)
 
 
 def update_call(core, master, moment, second, gradient, whole):
-    any_space = pl.BlockSpec(memory_space=pl.ANY)
     state = pl.BlockSpec((2, SUB_STEP, KVW), lambda i, core: (0, i, 0))
     half = pl.BlockSpec((SUB_STEP, KVW), lambda i, core: (i, 0))
+    part = pl.BlockSpec((ROWS, HALF // UPDATE_STEPS), lambda i, core: (0, i))
     shaped = [a.reshape(2, SUB, KVW) for a in (master, moment, second, gradient)]
     outs = pl.pallas_call(
         update_kernel,
         grid_spec=pltpu.PrefetchScalarGridSpec(
             num_scalar_prefetch=1,
             grid=(UPDATE_STEPS,),
-            in_specs=[state] * 4 + [any_space],
-            out_specs=[state] * 3 + [half] * 2 + [any_space] * 2,
-            scratch_shapes=[pltpu.SemaphoreType.DMA((8, 2))],
+            in_specs=[state] * 4
+            + [pl.BlockSpec((ROWS, D // UPDATE_STEPS), lambda i, core: (0, i))],
+            out_specs=[state] * 3 + [half] * 2 + [part] * 2,
         ),
         out_shape=[jax.ShapeDtypeStruct((2, SUB, KVW), jnp.float32)] * 3
         + [jax.ShapeDtypeStruct((SUB, KVW), jnp.bfloat16)] * 2
         + [jax.ShapeDtypeStruct((ROWS, HALF), jnp.bfloat16)] * 2,
         compiler_params=pltpu.CompilerParams(vmem_limit_bytes=VMEM),
-        cost_estimate=pl.CostEstimate(flops=0, bytes_accessed=23 << 20, transcendentals=0),
+        cost_estimate=COST,
         name="update",
     )(core, *shaped, whole)
     return [a.reshape(master.shape) for a in outs[:3]], *outs[3:]
@@ -223,11 +195,13 @@
     begun = take(1) if plan.adds else []
     after = take(plan.after)
     fresh = take(plan.blocks) if plan.last else []
+    kept = take(1) if plan.keeps else []
     out = take(1) if plan.after else []
     columns, column_sems = take(2)
     last_slots, last_sems = take(2) if plan.last else (None, None)
     after_slots, after_sems = take(2) if plan.after else (None, None)
     (store_sems,) = take(1) if plan.last else (None,)
+    (keep_sems,) = take(1) if plan.keeps else (None,)
 
     taken_up = range(plan.first, plan.first + plan.count)
     chunks = range(8) if plan.last else taken_up
@@ -268,6 +242,15 @@
         part = columns[chunk]
         if plan.last:
             last_reads[chunk].wait()
+            if plan.keeps:
+                stores.append(
+                    pltpu.make_async_copy(
+                        last_slots.at[chunk],
+                        kept[0].at[pl.ds(chunk * SUB, SUB)],
+                        keep_sems.at[chunk],
+                    )
+                )
+                stores[-1].start()
             update = lax.dot_general(
                 projected,
                 last_slots[chunk],
@@ -318,6 +301,7 @@
     adds: bool = False
     skip: int = 0
     swaps: bool = False
+    keeps: bool = False
     picks: bool = False
 
 
@@ -337,6 +321,9 @@
         out_shape += [jax.ShapeDtypeStruct((ROWS, HALF), jnp.bfloat16)] * plan.blocks
         out_specs += [any_space] * plan.blocks
         scratch += [pltpu.VMEM((8, SUB, KVW), jnp.bfloat16), pltpu.SemaphoreType.DMA((8,))]
+    if plan.keeps:
+        out_shape.append(jax.ShapeDtypeStruct((HALF, KVW), jnp.bfloat16))
+        out_specs.append(any_space)
     if plan.after:
         out_shape.append(jax.ShapeDtypeStruct((rows - plan.skip * ROWS, KVW + LANES), jnp.float32))
         out_specs.append(vmem)
@@ -346,9 +333,8 @@
         ]
     if plan.last:
         scratch.append(pltpu.SemaphoreType.DMA((8, plan.blocks)))
-    flops = 2 * SUB * KVW * (rows * 8 * (plan.last > 0) + (rows - plan.skip * ROWS) * count)
-    moved = (2 << 20) * plan.blocks * (1 + (plan.last > 0)) + (4 << 20) * (plan.last > 0)
-    moved += count << 19
+    if plan.keeps:
+        scratch.append(pltpu.SemaphoreType.DMA((8,)))
     return pl.pallas_call(
         functools.partial(layer_kernel, plan),
         in_specs=[pl.BlockSpec(memory_space=pltpu.SMEM)]
@@ -361,7 +347,7 @@
         out_shape=out_shape,
         scratch_shapes=scratch,
         compiler_params=pltpu.CompilerParams(vmem_limit_bytes=VMEM),
-        cost_estimate=pl.CostEstimate(flops=flops, bytes_accessed=moved, transcendentals=0),
+        cost_estimate=COST,
         name=name,
     )(table, *blocks, *sums, *last, *begun, *after)
 
@@ -434,9 +420,7 @@
             pltpu.SemaphoreType.DMA((16,)),
         ],
         compiler_params=pltpu.CompilerParams(vmem_limit_bytes=VMEM),
-        cost_estimate=pl.CostEstimate(
-            flops=2 * ROWS * D * KVW, bytes_accessed=16 << 20, transcendentals=0
-        ),
+        cost_estimate=COST,
         name="final_layer",
     )(table, keep, got, mine, theirs, *here, *there)
 
@@ -480,63 +464,60 @@
     home_own = [even_rows, to_ring(even_rows)]
     home_other = to_pair(even_rows)
     near_odd = to_chip(odd_rows, 1)
-    odd = to_next(jnp.where(upper, keep, got), 0)
 
     phase = (home_own[1], home_other, near_odd)
     home_own.append(to_ring(after(home_own[1], *phase)))
     home_others = [after(home_other, *phase)]
     home_others.append(to_ring(home_others[0]))
-    far = to_chip(after(near_odd, *phase), 1)
-    near_even = to_chip(after(even_rows, *phase), 1)
-
-    phase = (home_own[2], home_others[1], far)
+    near_odd = after(near_odd, *phase)
+    far = to_chip(near_odd, 1)
+    third_other = to_pair(near_odd)
+    odd = jnp.where(upper, keep, got)
+
+    phase = (home_own[2], home_others[1], far, third_other, odd)
     home_own.append(to_ring(after(home_own[2], *phase)))
     home_others.append(to_ring(after(home_others[1], *phase)))
     far = after(far, *phase)
     far_other = to_pair(far)
-
-    phase = (home_own[3], home_others[2], far_other, odd)
+    near_even = to_chip(after(even_rows, *phase), 1)
+    odd = to_chip(after(odd, *phase), 2)
+
+    phase = (home_own[3], home_others[2], far_other, near_even)
     home_others.append(to_ring(after(home_others[2], *phase)))
     first = [after(together(far, far_other), *phase)]
     first.append(to_ring(first[0]))
-    odd = to_next(after(odd, *phase), 1)
+    near_even = after(near_even, *phase)
+    second_other = to_pair(near_even)
+    third = [together(near_odd, third_other)]
 
     home = [piece for pair in zip(home_own, home_others) for piece in pair]
     (product,) = layer_call(table, (keep, got), after=home, picks=True, name="project_home")
-    phase = (first[1], home_others[3], near_even)
+    phase = (first[1], home_others[3], second_other)
     first.append(to_ring(after(first[1], *phase)))
-    second_own = [after(near_even, *phase)]
-    second_own.append(to_ring(second_own[0]))
-    second_others = [to_pair(second_own[0])]
-    (even,) = layer_call(
+    second = [after(together(near_even, second_other), *phase)]
+    second.append(to_ring(second[0]))
+    even, home_here = layer_call(
         table,
         (keep, got),
         sums=(product, to_core(after(product, *phase))),
         last=home,
         picks=True,
+        keeps=True,
         name="expand_home",
     )
-    even = to_next(even, 0)
-    third_other = to_pair(after(near_odd, even))
-
-    phase = (first[2], second_own[1], odd)
+    phase = (first[2], second[1], odd, even, third[0])
+    even = to_chip(even, 2)
+    home_there = to_core(after(home_here, *phase))
     first.append(to_ring(after(first[2], *phase)))
-    second_own.append(to_ring(after(second_own[1], *phase)))
-    second_others.append(to_pair(second_own[1]))
-    home_there = to_core(jnp.concatenate([after(piece, *phase) for piece in home], axis=0))
-
-    phase = (first[3], second_own[2], even, third_other, second_others[0])
-    even = to_next(after(even, *phase), 1)
-    third = [after(together(near_odd, third_other), *phase)]
-    third.append(to_ring(third[0]))
-    second_own.append(to_ring(after(second_own[2], *phase)))
-    second_others.append(to_pair(after(second_own[2], *phase)))
-
-    phase = (third[1], second_own[3], home_there, second_others[1])
+    second.append(to_ring(after(second[1], *phase)))
+
+    phase = (first[3], second[2])
+    second.append(to_ring(after(second[2], *phase)))
+    third.append(to_ring(after(third[0], *phase)))
+
+    even = after(even, second[3])
+    phase = (second[3], third[1], home_there)
     third.append(to_ring(after(third[1], *phase)))
-    second_others.append(to_pair(after(second_own[3], *phase)))
-    second = [piece for pair in zip(second_own, second_others) for piece in pair]
-    even = after(even, *phase, second_others[2])
     third.append(to_ring(third[2]))
 
     (product,) = layer_call(table, (even, odd), after=first, name="project_first")
@@ -564,13 +545,13 @@
         (even, odd),
         sums=(product, to_core(product)),
         last=third,
-        after=home,
+        after=[home_here],
         skip=1,
         swaps=True,
         name="third_home",
     )
     out = final_call(
-        table, keep, to_core(give), product, to_core(product), home, [home_there]
+        table, keep, to_core(give), product, to_core(product), [home_here], [home_there]
     )
     return (*states, out.reshape(hidden_states.shape))
 

time: 467 us -> 313 us (0.67)
  Pallas kernels: 198 us -> 78.3 us
  waiting for transfers between devices: 168 us -> 139 us
    pallas_call x1, Pallas kernels: 131 us -> 11.4 us  [update_call(): pl.pallas_call(update_kernel, grid_spec=pltpu.PrefetchScalarGridSpec(num_...]
    ppermute x38 -> x33, waiting for transfers between devices: 168 us -> 139 us  [shift(): return lax.ppermute(value, AXES, pairs)]
    ppermute x38 -> x33, starting transfers between devices: 81.1 us -> 81.2 us  [shift(): return lax.ppermute(value, AXES, pairs)]
  transfers between devices with their start and end apart: 38 -> 33, of which waited for: 21 -> 18; matrix products, arithmetic and copies ran while one was open for 1% -> 2% of each run, Pallas kernels for 8% -> 14%
where the time goes in v1:
time: 313 us
  waiting for transfers between devices  139 us (44%)
  starting transfers between devices  81.2 us (26%)
  Pallas kernels  78.3 us (25%)
  local copies, waits for them, and re-layouts  8.19 us (3%)
  other arithmetic  4.8 us (2%)
    ppermute x33, waiting for transfers between devices, shift(): return lax.ppermute(value, AXES, pairs)  139 us
    ppermute x33, starting transfers between devices, shift(): return lax.ppermute(value, AXES, pairs)  81.2 us
    pallas_call x7, Pallas kernels, layer_call(): pl.pallas_call(functools.partial(layer_kernel, plan), in_specs=[pl.BlockS...  57.8 us
    pallas_call x1, Pallas kernels, update_call(): pl.pallas_call(update_kernel, grid_spec=pltpu.PrefetchScalarGridSpec(num_...  11.4 us
    pallas_call x1, Pallas kernels, final_call(): pl.pallas_call(final_kernel, in_specs=[pl.BlockSpec(memory_space=pltpu.SM...  9.02 us
    unnamed x59, local copies, waits for them, and re-layouts  7.98 us
  transfers between devices with their start and end apart: 33, of which 18 were waited for; matrix products, arithmetic and copies ran while one was open for 2% of the time, Pallas kernels for 14%

profile of v1, /device:TPU:1, one launch (start us, length us, event | category | flops | bytes accessed | tf_op | source)
XLA Modules:
  0.0 312.5 jit_solution(6258699160531189489)
XLA Ops:
  0.6 11.4 %update.1 = (f32[2,512,512]{2,1,0:T(8,128)}, f32[2,512,512]{2,1,0:T(8,128)}, f32[2,512,512]{2,1,0:T(8,128)}, bf16[512,512]{1,0:T(8,128)(2,1)}, bf16[512,512]{1,0...) custom-call(s32[1]{0:T(128)} %bitcast.core_ref, f32[2,512,512]{2,1,0:T(8,128)} %bitcast.12, ...), custom_call_target="tpu_custom_call" | custom-call | flops 1 | bytes 1 | tf_op jit(solution)/shard_map/update/pallas_call | solution.py:112
  12.1 1.5 collective-permute-start
  13.6 1.7 collective-permute-done
  15.7 1.1 broadcast_select_fusion.1
  16.8 1.4 collective-permute-start.4
  18.3 3.8 %collective-permute-start.3 = (bf16[512,512]{1,0:T(8,128)(2,1)S(1)}, bf16[512,512]{1,0:T(8,128)(2,1)S(1)}, u32[]{:S(2)}, u32[]{:S(2)}) collective-permute-start(bf16[512,512]{1,0:T(8,128)(2,1)S(1)} %get-tuple-element.58.refs_3_.refs_5_), channel_id=1, source_target_pairs={{0,1},{1,2},{2,3},{3,0},{4,5},{5,6},{6,7},{7,4},{8,11},{9,8},{10,9... | collective-permute-start | bytes 1572872 | tf_op jit(solution)/shard_map/ppermute | solution.py:45
  22.0 1.2 collective-permute-start.2
  23.2 11.1 %collective-permute-done.4 = bf16[512,512]{1,0:T(8,128)(2,1)S(1)} collective-permute-done((bf16[512,512]{1,0:T(8,128)(2,1)S(1)}, bf16[512,512]{1,0:T(8,128)(2,1)S(1)}, u32[]{:S(2)}, u32[]{:S(2)}) %collective-permute-start.4) | collective-permute-done | bytes 524320 | tf_op jit(solution)/shard_map/ppermute | solution.py:45
  35.0 1.3 collective-permute-start.8
  37.2 1.8 collective-permute-start.5
  39.2 1.6 broadcast_select_fusion
  40.8 4.8 %collective-permute-done.5.refs_6_.refs_8_ = bf16[512,512]{1,0:T(8,128)(2,1)S(1)} collective-permute-done((bf16[512,512]{1,0:T(8,128)(2,1)S(1)}, bf16[512,512]{1,0:T(8,128)(2,1)S(1)}, u32[]{:S(2)}, u32[]{:S(2)}) %collective-permute-start.5) | collective-permute-done | bytes 524320 | tf_op jit(solution)/shard_map/ppermute | solution.py:45
  45.6 5.6 %collective-permute-done.6.refs_7_.refs_9_ = bf16[512,512]{1,0:T(8,128)(2,1)S(1)} collective-permute-done((bf16[512,512]{1,0:T(8,128)(2,1)S(1)}, bf16[512,512]{1,0:T(8,128)(2,1)S(1)}, u32[]{:S(2)}, u32[]{:S(2)}) %collective-permute-start.6) | collective-permute-done | bytes 524320 | tf_op jit(solution)/shard_map/ppermute | solution.py:45
  51.2 18.4 %collective-permute-done.7 = bf16[512,512]{1,0:T(8,128)(2,1)S(1)} collective-permute-done((bf16[512,512]{1,0:T(8,128)(2,1)S(1)}, bf16[512,512]{1,0:T(8,128)(2,1)S(1)}, u32[]{:S(2)}, u32[]{:S(2)}) %collective-permute-start.7) | collective-permute-done | bytes 524320 | tf_op jit(solution)/shard_map/ppermute | solution.py:45
  70.1 3.8 %collective-permute-start.9 = (bf16[512,512]{1,0:T(8,128)(2,1)S(1)}, bf16[512,512]{1,0:T(8,128)(2,1)}, u32[]{:S(2)}, u32[]{:S(2)}) collective-permute-start(bf16[512,512]{1,0:T(8,128)(2,1)S(1)} %collective-permute-done.5.refs_6_.refs_8_), channel_id=1, source_target_pairs={{0,1},{1,2},{2,3},{3,0},{4,5},{5,6},{6,7},{7,4},{8,11},{9,8},{10,9... | collective-permute-start | bytes 1572872 | tf_op jit(solution)/shard_map/ppermute | solution.py:45
  74.0 7.5 %collective-permute-done.11 = bf16[512,512]{1,0:T(8,128)(2,1)S(1)} collective-permute-done((bf16[512,512]{1,0:T(8,128)(2,1)S(1)}, bf16[512,512]{1,0:T(8,128)(2,1)S(1)}, u32[]{:S(2)}, u32[]{:S(2)}) %collective-permute-start.11) | collective-permute-done | bytes 524320 | tf_op jit(solution)/shard_map/ppermute | solution.py:45
  81.6 4.1 %collective-permute-done.10.refs_9_.refs_11_ = bf16[512,512]{1,0:T(8,128)(2,1)S(1)} collective-permute-done((bf16[512,512]{1,0:T(8,128)(2,1)S(1)}, bf16[512,512]{1,0:T(8,128)(2,1)S(1)}, u32[]{:S(2)}, u32[]{:S(2)}) %collective-permute-start.10) | collective-permute-done | bytes 524320 | tf_op jit(solution)/shard_map/ppermute | solution.py:45
  85.6 6.0 %collective-permute-done.12 = bf16[512,512]{1,0:T(8,128)(2,1)S(1)} collective-permute-done((bf16[512,512]{1,0:T(8,128)(2,1)S(1)}, bf16[512,512]{1,0:T(8,128)(2,1)S(1)}, u32[]{:S(2)}, u32[]{:S(2)}) %collective-permute-start.12) | collective-permute-done | bytes 524320 | tf_op jit(solution)/shard_map/ppermute | solution.py:45
  91.7 2.8 collective-permute-start.14
  94.5 1.7 collective-permute-start.15
  96.3 9.8 %collective-permute-done.15 = bf16[512,512]{1,0:T(8,128)(2,1)} collective-permute-done((bf16[512,512]{1,0:T(8,128)(2,1)S(1)}, bf16[512,512]{1,0:T(8,128)(2,1)}, u32[]{:S(2)}, u32[]{:S(2)}) %collective-permute-start.15) | collective-permute-done | bytes 524320 | tf_op jit(solution)/shard_map/ppermute | solution.py:45
  106.1 1.3 pad_maximum_fusion.1.refs_9_.refs_5_
  107.4 4.5 %collective-permute-done.13.refs_10_.refs_12_ = bf16[512,512]{1,0:T(8,128)(2,1)} collective-permute-done((bf16[512,512]{1,0:T(8,128)(2,1)}, bf16[512,512]{1,0:T(8,128)(2,1)}, u32[]{:S(2)}, u32[]{:S(2)}) %collective-permute-start.13) | collective-permute-done | bytes 524320 | tf_op jit(solution)/shard_map/ppermute | solution.py:45
  111.9 3.4 %collective-permute-start.18 = (bf16[1024,512]{1,0:T(8,128)(2,1)S(1)}, bf16[1024,512]{1,0:T(8,128)(2,1)}, u32[]{:S(2)}, u32[]{:S(2)}) collective-permute-start(bf16[1024,512]{1,0:T(8,128)(2,1)S(1)} %pad_maximum_fusion.1.refs_9_.refs_5_), channel_id=1, source_target_pairs={{0,1},{1,2},{2,3},{3,0},{4,5},{5,6},{6,7},{7,4},{8,11},{9,8},{10,9... | collective-permute-start | bytes 3145736 | tf_op jit(solution)/shard_map/ppermute | solution.py:45
  116.4 5.3 %project_home.1.refs_3_ = f32[256,640]{1,0:T(8,128)} custom-call(s32[24]{0:T(128)} %pad_add_fusion.refs_0_.table, bf16[256,4096]{1,0:T(8,128)(2,1)} %get-tuple-element.47.refs_1_, bf16[256,4096]{1,0:T(8,128)(2,1)} %collective-permute-done.1.refs_2_, bf16[512,512]{1,0:T(8,128)(2,1)} %copy-done.5, bf16[512,512]{1,0:T(8,128)(2,1)} %copy-done.14, ...), custom_call_target="tpu_custom_call" | custom-call | flops 1 | bytes 1 | tf_op jit(solution)/shard_map/project_home/pallas_call | solution.py:338
  121.7 5.0 %collective-permute-start.16 = (f32[256,640]{1,0:T(8,128)}, f32[256,640]{1,0:T(8,128)S(1)}, u32[]{:S(2)}, u32[]{:S(2)}) collective-permute-start(f32[256,640]{1,0:T(8,128)} %project_home.1.refs_3_), channel_id=1, source_target_pairs={{0,8},{1,9},{2,10},{3,11},{4,12},{5,13},{6,14},{7,15},{8,0},{9,1},... | collective-permute-start | bytes 1966088 | tf_op jit(solution)/shard_map/ppermute | solution.py:45
  126.8 1.8 collective-permute-done.16.refs_4_
  129.5 7.3 %expand_home.1 = (bf16[256,4096]{1,0:T(8,128)(2,1)}, bf16[4096,512]{1,0:T(8,128)(2,1)}) custom-call(s32[24]{0:T(128)} %pad_add_fusion.refs_0_.table, bf16[256,4096]{1,0:T(8,128)(2,1)} %get-tuple-element.47.refs_1_, bf16[256,4096]{1,0:T(8,128)(2,1)} %collective-permute-done.1.refs_2_, f32[256,640]{1,0:T(8,128)} %project_home.1.refs_3_, ...), custom_call_target="tpu_custom_call" | custom-call | flops 1 | bytes 1 | tf_op jit(solution)/shard_map/expand_home/pallas_call | solution.py:338
  136.8 6.0 %collective-permute-done.20.refs_2_ = bf16[256,4096]{1,0:T(8,128)(2,1)} collective-permute-done((bf16[256,4096]{1,0:T(8,128)(2,1)}, bf16[256,4096]{1,0:T(8,128)(2,1)}, u32[]{:S(2)}, u32[]{:S(2)}) %collective-permute-start.20) | collective-permute-done | bytes 2097184 | tf_op jit(solution)/shard_map/ppermute | solution.py:45
  142.8 7.5 %collective-permute-start.27 = (bf16[4096,512]{1,0:T(8,128)(2,1)}, bf16[4096,512]{1,0:T(8,128)(2,1)}, u32[]{:S(2)}, u32[]{:S(2)}) collective-permute-start(bf16[4096,512]{1,0:T(8,128)(2,1)} %get-tuple-element.76.refs_9_.refs_0_), channel_id=1, source_target_pairs={{0,8},{1,9},{2,10},{3,11},{4,12},{5,13},{6,14},{7,15},{8,0},{9,1},... | collective-permute-start | bytes 12582920 | tf_op jit(solution)/shard_map/ppermute | solution.py:45
  150.3 2.2 collective-permute-start.21
  153.0 33.5 %collective-permute-start.17 = (bf16[256,4096]{1,0:T(8,128)(2,1)}, bf16[256,4096]{1,0:T(8,128)(2,1)S(1)}, u32[]{:S(2)}, u32[]{:S(2)}) collective-permute-start(bf16[256,4096]{1,0:T(8,128)(2,1)} %get-tuple-element.63), channel_id=1, source_target_pairs={{0,32},{1,33},{2,34},{3,35},{4,36},{5,37},{6,38},{7,39},{8,40},{9,... | collective-permute-start | bytes 6291464 | tf_op jit(solution)/shard_map/ppermute | solution.py:45
  187.1 3.0 collective-permute-start.26
  190.1 45.0 %collective-permute-done.17.refs_1_ = bf16[256,4096]{1,0:T(8,128)(2,1)S(1)} collective-permute-done((bf16[256,4096]{1,0:T(8,128)(2,1)}, bf16[256,4096]{1,0:T(8,128)(2,1)S(1)}, u32[]{:S(2)}, u32[]{:S(2)}) %collective-permute-start.17) | collective-permute-done | bytes 2097184 | tf_op jit(solution)/shard_map/ppermute | solution.py:45
  235.1 1.3 copy-done.3
  236.4 6.4 %project_first.1.refs_3_ = f32[512,640]{1,0:T(8,128)} custom-call(s32[24]{0:T(128)} %pad_add_fusion.refs_0_.table, bf16[256,4096]{1,0:T(8,128)(2,1)} %copy-done.3, bf16[256,4096]{1,0:T(8,128)(2,1)} %collective-permute-done.20.refs_2_, bf16[1024,512]{1,0:T(8,128)(2,1)} %copy-done.1, bf16[1024,512]{1,0:T(8,128)(2,1)} %copy-done.6, ...), custom_call_target="tpu_custom_call" | custom-call | flops 1 | bytes 1 | tf_op jit(solution)/shard_map/project_first/pallas_call | solution.py:338
  244.2 2.2 collective-permute-done.24.refs_4_
  246.4 1.1 copy-done.19
  247.5 11.9 %first_second.1 = (bf16[256,4096]{1,0:T(8,128)(2,1)}, bf16[256,4096]{1,0:T(8,128)(2,1)}, f32[512,640]{1,0:T(8,128)}) custom-call(s32[24]{0:T(128)} %pad_add_fusion.refs_0_.table, bf16[256,4096]{1,0:T(8,128)(2,1)} %copy-done.3, bf16[256,4096]{1,0:T(8,128)(2,1)} %collective-permute-done.20.refs_2_, f32[512,640]{1,0:T(8,128)} %project_first.1.refs_3_, ...), custom_call_target="tpu_custom_call" | custom-call | flops 1 | bytes 1 | tf_op jit(solution)/shard_map/first_second/pallas_call | solution.py:338
  260.5 2.2 collective-permute-done.25.refs_4_
  262.7 1.1 copy-done.21
  263.7 11.7 %second_third.1 = (bf16[256,4096]{1,0:T(8,128)(2,1)}, bf16[256,4096]{1,0:T(8,128)(2,1)}, f32[512,640]{1,0:T(8,128)}) custom-call(s32[24]{0:T(128)} %pad_add_fusion.refs_0_.table, bf16[256,4096]{1,0:T(8,128)(2,1)} %get-tuple-element.71.refs_1_, bf16[256,4096]{1,0:T(8,128)(2,1)} %get-tuple-element.72.refs_2_, f32[512,640]{1,0:T(8,128)} %get-tuple-element.73.refs_3_, ...), custom_call_target="tpu_custom_call" | custom-call | flops 1 | bytes 1 | tf_op jit(solution)/shard_map/second_third/pallas_call | solution.py:338
  276.4 4.6 %third_rest.1.refs_3_ = f32[512,640]{1,0:T(8,128)} custom-call(s32[24]{0:T(128)} %pad_add_fusion.refs_0_.table, bf16[256,4096]{1,0:T(8,128)(2,1)} %get-tuple-element.78.refs_1_, bf16[256,4096]{1,0:T(8,128)(2,1)} %get-tuple-element.79.refs_2_, f32[512,640]{1,0:T(8,128)} %get-tuple-element.80.refs_3_, bf16[1024,512]{1,0:T(8,128)(2,1)} %copy-done.8), custom_call_target="tpu_custom_call" | custom-call | flops 1 | bytes 1 | tf_op jit(solution)/shard_map/third_rest/pallas_call | solution.py:338
  281.8 2.9 collective-permute-done.30.refs_4_
  284.6 1.1 copy-done.20
  285.7 10.6 %third_home.1 = (bf16[256,4096]{1,0:T(8,128)(2,1)}, bf16[256,4096]{1,0:T(8,128)(2,1)}, f32[256,640]{1,0:T(8,128)}) custom-call(s32[24]{0:T(128)} %pad_add_fusion.refs_0_.table, bf16[256,4096]{1,0:T(8,128)(2,1)} %get-tuple-element.78.refs_1_, bf16[256,4096]{1,0:T(8,128)(2,1)} %get-tuple-element.79.refs_2_, f32[512,640]{1,0:T(8,128)} %third_rest.1.refs_3_, ...), custom_call_target="tpu_custom_call" | custom-call | flops 1 | bytes 1 | tf_op jit(solution)/shard_map/third_home/pallas_call | solution.py:338
  296.9 4.8 %collective-permute-done.32.theirs = f32[256,640]{1,0:T(8,128)S(1)} collective-permute-done((f32[256,640]{1,0:T(8,128)}, f32[256,640]{1,0:T(8,128)S(1)}, u32[]{:S(2)}, u32[]{:S(2)}) %collective-permute-start.32) | collective-permute-done | bytes 655392 | tf_op jit(solution)/shard_map/ppermute | solution.py:45
  303.3 9.0 %final_layer.1 = bf16[256,8192]{1,0:T(8,128)(2,1)} custom-call(s32[24]{0:T(128)} %pad_add_fusion.refs_0_.table, bf16[256,4096]{1,0:T(8,128)(2,1)} %get-tuple-element.81.keep, bf16[256,4096]{1,0:T(8,128)(2,1)} %copy-done.18, f32[256,640]{1,0:T(8,128)} %get-tuple-element.83.mine, f32[256,640]{1,0:T(8,128)} %copy-done.23, ...), custom_call_target="tpu_custom_call" | custom-call | flops 1 | bytes 1 | tf_op jit(solution)/shard_map/final_layer/pallas_call | solution.py:409
  (99 shorter events, 12.6 us)
Async XLA Ops:
  12.1 27.1 %copy-start = (bf16[256,4096]{1,0:T(8,128)(2,1)S(1)}, bf16[256,4096]{1,0:T(8,128)(2,1)}, u32[]{:S(2)}) copy-start(bf16[256,4096]{1,0:T(8,128)(2,1)} %get-tuple-element.47.refs_1_) | copy-start | bytes 6291460
  12.1 3.2 %collective-permute-start = (bf16[512,512]{1,0:T(8,128)(2,1)}, bf16[512,512]{1,0:T(8,128)(2,1)S(1)}, u32[]{:S(2)}, u32[]{:S(2)}) collective-permute-start(bf16[512,512]{1,0:T(8,128)(2,1)} %get-tuple-element.49), channel_id=1, source_target_pairs={{0,8},{1,9},{2,10},{3,11},{4,12},{5,13},{6,14},{7,15},{8,0},{9,1},... | collective-permute-start | bytes 1572872 | tf_op jit(solution)/shard_map/ppermute | solution.py:45
  15.3 23.9 %collective-permute-start.1 = (bf16[256,4096]{1,0:T(8,128)(2,1)}, bf16[256,4096]{1,0:T(8,128)(2,1)}, u32[]{:S(2)}, u32[]{:S(2)}) collective-permute-start(bf16[256,4096]{1,0:T(8,128)(2,1)} %get-tuple-element.50), channel_id=1, source_target_pairs={{0,8},{1,9},{2,10},{3,11},{4,12},{5,13},{6,14},{7,15},{8,0},{9,1},... | collective-permute-start | bytes 6291464 | tf_op jit(solution)/shard_map/ppermute | solution.py:45
  16.8 57.2 %copy-start.5 = (bf16[512,512]{1,0:T(8,128)(2,1)}, bf16[512,512]{1,0:T(8,128)(2,1)S(1)}, u32[]{:S(2)}) copy-start(bf16[512,512]{1,0:T(8,128)(2,1)S(1)} %get-tuple-element.58.refs_3_.refs_5_) | copy-start | bytes 1572868
  16.8 17.5 %collective-permute-start.4 = (bf16[512,512]{1,0:T(8,128)(2,1)S(1)}, bf16[512,512]{1,0:T(8,128)(2,1)S(1)}, u32[]{:S(2)}, u32[]{:S(2)}) collective-permute-start(bf16[512,512]{1,0:T(8,128)(2,1)S(1)} %get-tuple-element.84), channel_id=1, source_target_pairs={{0,16},{1,17},{2,18},{3,19},{4,20},{5,21},{6,22},{7,23},{8,24},{9,... | collective-permute-start | bytes 1572872 | tf_op jit(solution)/shard_map/ppermute | solution.py:45
  18.3 16.1 %collective-permute-start.3 = (bf16[512,512]{1,0:T(8,128)(2,1)S(1)}, bf16[512,512]{1,0:T(8,128)(2,1)S(1)}, u32[]{:S(2)}, u32[]{:S(2)}) collective-permute-start(bf16[512,512]{1,0:T(8,128)(2,1)S(1)} %get-tuple-element.58.refs_3_.refs_5_), channel_id=1, source_target_pairs={{0,1},{1,2},{2,3},{3,0},{4,5},{5,6},{6,7},{7,4},{8,11},{9,8},{10,9... | collective-permute-start | bytes 1572872 | tf_op jit(solution)/shard_map/ppermute | solution.py:45
  22.0 12.9 %collective-permute-start.2 = (bf16[512,512]{1,0:T(8,128)(2,1)S(1)}, bf16[512,512]{1,0:T(8,128)(2,1)S(1)}, u32[]{:S(2)}, u32[]{:S(2)}) collective-permute-start(bf16[512,512]{1,0:T(8,128)(2,1)S(1)} %get-tuple-element.58.refs_3_.refs_5_), channel_id=1, source_target_pairs={{0,4},{1,5},{2,6},{3,7},{4,0},{5,1},{6,2},{7,3},{8,12},{9,13},{10,... | collective-permute-start | bytes 1572872 | tf_op jit(solution)/shard_map/ppermute | solution.py:45
  35.0 16.2 %collective-permute-start.8 = (bf16[512,512]{1,0:T(8,128)(2,1)S(1)}, bf16[512,512]{1,0:T(8,128)(2,1)S(1)}, u32[]{:S(2)}, u32[]{:S(2)}) collective-permute-start(bf16[512,512]{1,0:T(8,128)(2,1)S(1)} %collective-permute-done.4), channel_id=1, source_target_pairs={{0,4},{1,5},{2,6},{3,7},{4,0},{5,1},{6,2},{7,3},{8,12},{9,13},{10,... | collective-permute-start | bytes 1572872 | tf_op jit(solution)/shard_map/ppermute | solution.py:45
  36.2 33.3 %collective-permute-start.7 = (bf16[512,512]{1,0:T(8,128)(2,1)S(1)}, bf16[512,512]{1,0:T(8,128)(2,1)S(1)}, u32[]{:S(2)}, u32[]{:S(2)}) collective-permute-start(bf16[512,512]{1,0:T(8,128)(2,1)S(1)} %collective-permute-done.4), channel_id=1, source_target_pairs={{0,16},{1,17},{2,18},{3,19},{4,20},{5,21},{6,22},{7,23},{8,24},{9,... | collective-permute-start | bytes 1572872 | tf_op jit(solution)/shard_map/ppermute | solution.py:45
  37.2 8.3 %collective-permute-start.5 = (bf16[512,512]{1,0:T(8,128)(2,1)S(1)}, bf16[512,512]{1,0:T(8,128)(2,1)S(1)}, u32[]{:S(2)}, u32[]{:S(2)}) collective-permute-start(bf16[512,512]{1,0:T(8,128)(2,1)S(1)} %collective-permute-done.2.refs_4_.refs_6_), channel_id=1, source_target_pairs={{0,1},{1,2},{2,3},{3,0},{4,5},{5,6},{6,7},{7,4},{8,11},{9,8},{10,9... | collective-permute-start | bytes 1572872 | tf_op jit(solution)/shard_map/ppermute | solution.py:45
  39.1 12.1 %collective-permute-start.6 = (bf16[512,512]{1,0:T(8,128)(2,1)S(1)}, bf16[512,512]{1,0:T(8,128)(2,1)S(1)}, u32[]{:S(2)}, u32[]{:S(2)}) collective-permute-start(bf16[512,512]{1,0:T(8,128)(2,1)S(1)} %collective-permute-done.3.refs_5_.refs_7_), channel_id=1, source_target_pairs={{0,1},{1,2},{2,3},{3,0},{4,5},{5,6},{6,7},{7,4},{8,11},{9,8},{10,9... | collective-permute-start | bytes 1572872 | tf_op jit(solution)/shard_map/ppermute | solution.py:45
  45.6 46.1 %copy-start.15 = (bf16[512,512]{1,0:T(8,128)(2,1)}, bf16[512,512]{1,0:T(8,128)(2,1)S(1)}, u32[]{:S(2)}) copy-start(bf16[512,512]{1,0:T(8,128)(2,1)S(1)} %collective-permute-done.5.refs_6_.refs_8_) | copy-start | bytes 1572868
  51.2 43.3 %copy-start.16 = (bf16[512,512]{1,0:T(8,128)(2,1)}, bf16[512,512]{1,0:T(8,128)(2,1)S(1)}, u32[]{:S(2)}) copy-start(bf16[512,512]{1,0:T(8,128)(2,1)S(1)} %collective-permute-done.6.refs_7_.refs_9_) | copy-start | bytes 1572868
  51.2 45.0 %copy-start.26 = (bf16[512,512]{1,0:T(8,128)(2,1)}, bf16[512,512]{1,0:T(8,128)(2,1)S(1)}, u32[]{:S(2)}) copy-start(bf16[512,512]{1,0:T(8,128)(2,1)S(1)} %collective-permute-done.8) | copy-start | bytes 1572868
  69.6 11.9 %collective-permute-start.11 = (bf16[512,512]{1,0:T(8,128)(2,1)S(1)}, bf16[512,512]{1,0:T(8,128)(2,1)S(1)}, u32[]{:S(2)}, u32[]{:S(2)}) collective-permute-start(bf16[512,512]{1,0:T(8,128)(2,1)S(1)} %collective-permute-done.7), channel_id=1, source_target_pairs={{0,4},{1,5},{2,6},{3,7},{4,0},{5,1},{6,2},{7,3},{8,12},{9,13},{10,... | collective-permute-start | bytes 1572872 | tf_op jit(solution)/shard_map/ppermute | solution.py:45
  70.1 11.4 %collective-permute-start.9 = (bf16[512,512]{1,0:T(8,128)(2,1)S(1)}, bf16[512,512]{1,0:T(8,128)(2,1)}, u32[]{:S(2)}, u32[]{:S(2)}) collective-permute-start(bf16[512,512]{1,0:T(8,128)(2,1)S(1)} %collective-permute-done.5.refs_6_.refs_8_), channel_id=1, source_target_pairs={{0,1},{1,2},{2,3},{3,0},{4,5},{5,6},{6,7},{7,4},{8,11},{9,8},{10,9... | collective-permute-start | bytes 1572872 | tf_op jit(solution)/shard_map/ppermute | solution.py:45
  73.9 11.7 %collective-permute-start.10 = (bf16[512,512]{1,0:T(8,128)(2,1)S(1)}, bf16[512,512]{1,0:T(8,128)(2,1)S(1)}, u32[]{:S(2)}, u32[]{:S(2)}) collective-permute-start(bf16[512,512]{1,0:T(8,128)(2,1)S(1)} %collective-permute-done.6.refs_7_.refs_9_), channel_id=1, source_target_pairs={{0,1},{1,2},{2,3},{3,0},{4,5},{5,6},{6,7},{7,4},{8,11},{9,8},{10,9... | collective-permute-start | bytes 1572872 | tf_op jit(solution)/shard_map/ppermute | solution.py:45
  74.0 17.6 %collective-permute-start.12 = (bf16[512,512]{1,0:T(8,128)(2,1)S(1)}, bf16[512,512]{1,0:T(8,128)(2,1)S(1)}, u32[]{:S(2)}, u32[]{:S(2)}) collective-permute-start(bf16[512,512]{1,0:T(8,128)(2,1)S(1)} %get-tuple-element.58.refs_3_.refs_5_), channel_id=1, source_target_pairs={{0,16},{1,17},{2,18},{3,19},{4,20},{5,21},{6,22},{7,23},{8,24},{9,... | collective-permute-start | bytes 1572872 | tf_op jit(solution)/shard_map/ppermute | solution.py:45
  81.6 40.1 %copy-start.1 = (bf16[1024,512]{1,0:T(8,128)(2,1)}, bf16[1024,512]{1,0:T(8,128)(2,1)S(1)}, u32[]{:S(2)}) copy-start(bf16[1024,512]{1,0:T(8,128)(2,1)S(1)} %pad_maximum_fusion.refs_3_.refs_5_) | copy-start | bytes 3145732
  85.6 8.8 %copy-start.17 = (bf16[512,512]{1,0:T(8,128)(2,1)}, bf16[512,512]{1,0:T(8,128)(2,1)S(1)}, u32[]{:S(2)}) copy-start(bf16[512,512]{1,0:T(8,128)(2,1)S(1)} %collective-permute-done.10.refs_9_.refs_11_) | copy-start | bytes 1572868
  91.7 20.3 %collective-permute-start.14 = (bf16[1024,512]{1,0:T(8,128)(2,1)S(1)}, bf16[1024,512]{1,0:T(8,128)(2,1)S(1)}, u32[]{:S(2)}, u32[]{:S(2)}) collective-permute-start(bf16[1024,512]{1,0:T(8,128)(2,1)S(1)} %pad_maximum_fusion.refs_3_.refs_5_), channel_id=1, source_target_pairs={{0,1},{1,2},{2,3},{3,0},{4,5},{5,6},{6,7},{7,4},{8,11},{9,8},{10,9... | collective-permute-start | bytes 3145736 | tf_op jit(solution)/shard_map/ppermute | solution.py:45
  94.5 48.3 %collective-permute-start.20 = (bf16[256,4096]{1,0:T(8,128)(2,1)}, bf16[256,4096]{1,0:T(8,128)(2,1)}, u32[]{:S(2)}, u32[]{:S(2)}) collective-permute-start(bf16[256,4096]{1,0:T(8,128)(2,1)} %broadcast_select_fusion), channel_id=1, source_target_pairs={{0,32},{1,33},{2,34},{3,35},{4,36},{5,37},{6,38},{7,39},{8,40},{9,... | collective-permute-start | bytes 6291464 | tf_op jit(solution)/shard_map/ppermute | solution.py:45
  94.5 11.7 %collective-permute-start.15 = (bf16[512,512]{1,0:T(8,128)(2,1)S(1)}, bf16[512,512]{1,0:T(8,128)(2,1)}, u32[]{:S(2)}, u32[]{:S(2)}) collective-permute-start(bf16[512,512]{1,0:T(8,128)(2,1)S(1)} %collective-permute-done.12), channel_id=1, source_target_pairs={{0,4},{1,5},{2,6},{3,7},{4,0},{5,1},{6,2},{7,3},{8,12},{9,13},{10,... | collective-permute-start | bytes 1572872 | tf_op jit(solution)/shard_map/ppermute | solution.py:45
  96.2 15.8 %collective-permute-start.13 = (bf16[512,512]{1,0:T(8,128)(2,1)}, bf16[512,512]{1,0:T(8,128)(2,1)}, u32[]{:S(2)}, u32[]{:S(2)}) collective-permute-start(bf16[512,512]{1,0:T(8,128)(2,1)} %collective-permute-done.9.refs_8_.refs_10_), channel_id=1, source_target_pairs={{0,1},{1,2},{2,3},{3,0},{4,5},{5,6},{6,7},{7,4},{8,11},{9,8},{10,9... | collective-permute-start | bytes 1572872 | tf_op jit(solution)/shard_map/ppermute | solution.py:45
  107.4 14.3 %copy-start.2 = (bf16[1024,512]{1,0:T(8,128)(2,1)}, bf16[1024,512]{1,0:T(8,128)(2,1)S(1)}, u32[]{:S(2)}) copy-start(bf16[1024,512]{1,0:T(8,128)(2,1)S(1)} %pad_maximum_fusion.1.refs_9_.refs_5_) | copy-start | bytes 3145732
  111.9 9.8 %copy-start.6 = (bf16[1024,512]{1,0:T(8,128)(2,1)}, bf16[1024,512]{1,0:T(8,128)(2,1)S(1)}, u32[]{:S(2)}) copy-start(bf16[1024,512]{1,0:T(8,128)(2,1)S(1)} %collective-permute-done.14.refs_4_.refs_6_) | copy-start | bytes 3145732
  111.9 30.9 %collective-permute-start.18 = (bf16[1024,512]{1,0:T(8,128)(2,1)S(1)}, bf16[1024,512]{1,0:T(8,128)(2,1)}, u32[]{:S(2)}, u32[]{:S(2)}) collective-permute-start(bf16[1024,512]{1,0:T(8,128)(2,1)S(1)} %pad_maximum_fusion.1.refs_9_.refs_5_), channel_id=1, source_target_pairs={{0,1},{1,2},{2,3},{3,0},{4,5},{5,6},{6,7},{7,4},{8,11},{9,8},{10,9... | collective-permute-start | bytes 3145736 | tf_op jit(solution)/shard_map/ppermute | solution.py:45
  115.4 27.4 %collective-permute-start.19 = (bf16[1024,512]{1,0:T(8,128)(2,1)S(1)}, bf16[1024,512]{1,0:T(8,128)(2,1)}, u32[]{:S(2)}, u32[]{:S(2)}) collective-permute-start(bf16[1024,512]{1,0:T(8,128)(2,1)S(1)} %collective-permute-done.14.refs_4_.refs_6_), channel_id=1, source_target_pairs={{0,1},{1,2},{2,3},{3,0},{4,5},{5,6},{6,7},{7,4},{8,11},{9,8},{10,9... | collective-permute-start | bytes 3145736 | tf_op jit(solution)/shard_map/ppermute | solution.py:45
  116.4 10.3 %copy-start.25 = (bf16[512,512]{1,0:T(8,128)(2,1)S(1)}, bf16[512,512]{1,0:T(8,128)(2,1)}, u32[]{:S(2)}) copy-start(bf16[512,512]{1,0:T(8,128)(2,1)} %copy-done.24) | copy-start | bytes 1572868
  116.4 10.4 %copy-start.27 = (bf16[512,512]{1,0:T(8,128)(2,1)S(1)}, bf16[512,512]{1,0:T(8,128)(2,1)}, u32[]{:S(2)}) copy-start(bf16[512,512]{1,0:T(8,128)(2,1)} %copy-done.26) | copy-start | bytes 1572868
  121.7 6.9 %collective-permute-start.16 = (f32[256,640]{1,0:T(8,128)}, f32[256,640]{1,0:T(8,128)S(1)}, u32[]{:S(2)}, u32[]{:S(2)}) collective-permute-start(f32[256,640]{1,0:T(8,128)} %project_home.1.refs_3_), channel_id=1, source_target_pairs={{0,8},{1,9},{2,10},{3,11},{4,12},{5,13},{6,14},{7,15},{8,0},{9,1},... | collective-permute-start | bytes 1966088 | tf_op jit(solution)/shard_map/ppermute | solution.py:45
  126.8 60.4 %copy-start.4 = (bf16[1024,512]{1,0:T(8,128)(2,1)}, bf16[1024,512]{1,0:T(8,128)(2,1)S(1)}, u32[]{:S(2)}) copy-start(bf16[1024,512]{1,0:T(8,128)(2,1)S(1)} %constant_dynamic-update-slice_fusion.refs_9_.refs_5_) | copy-start | bytes 3145732
  142.8 100.7 %collective-permute-start.27 = (bf16[4096,512]{1,0:T(8,128)(2,1)}, bf16[4096,512]{1,0:T(8,128)(2,1)}, u32[]{:S(2)}, u32[]{:S(2)}) collective-permute-start(bf16[4096,512]{1,0:T(8,128)(2,1)} %get-tuple-element.76.refs_9_.refs_0_), channel_id=1, source_target_pairs={{0,8},{1,9},{2,10},{3,11},{4,12},{5,13},{6,14},{7,15},{8,0},{9,1},... | collective-permute-start | bytes 12582920 | tf_op jit(solution)/shard_map/ppermute | solution.py:45
  150.3 36.2 %collective-permute-start.21 = (bf16[1024,512]{1,0:T(8,128)(2,1)}, bf16[1024,512]{1,0:T(8,128)(2,1)S(1)}, u32[]{:S(2)}, u32[]{:S(2)}) collective-permute-start(bf16[1024,512]{1,0:T(8,128)(2,1)} %collective-permute-done.18.refs_10_.refs_6_), channel_id=1, source_target_pairs={{0,1},{1,2},{2,3},{3,0},{4,5},{5,6},{6,7},{7,4},{8,11},{9,8},{10,9... | collective-permute-start | bytes 3145736 | tf_op jit(solution)/shard_map/ppermute | solution.py:45
  152.5 34.0 %collective-permute-start.22 = (bf16[1024,512]{1,0:T(8,128)(2,1)}, bf16[1024,512]{1,0:T(8,128)(2,1)S(1)}, u32[]{:S(2)}, u32[]{:S(2)}) collective-permute-start(bf16[1024,512]{1,0:T(8,128)(2,1)} %collective-permute-done.19.refs_5_.refs_7_), channel_id=1, source_target_pairs={{0,1},{1,2},{2,3},{3,0},{4,5},{5,6},{6,7},{7,4},{8,11},{9,8},{10,9... | collective-permute-start | bytes 3145736 | tf_op jit(solution)/shard_map/ppermute | solution.py:45
  153.0 82.1 %collective-permute-start.17 = (bf16[256,4096]{1,0:T(8,128)(2,1)}, bf16[256,4096]{1,0:T(8,128)(2,1)S(1)}, u32[]{:S(2)}, u32[]{:S(2)}) collective-permute-start(bf16[256,4096]{1,0:T(8,128)(2,1)} %get-tuple-element.63), channel_id=1, source_target_pairs={{0,32},{1,33},{2,34},{3,35},{4,36},{5,37},{6,38},{7,39},{8,40},{9,... | collective-permute-start | bytes 6291464 | tf_op jit(solution)/shard_map/ppermute | solution.py:45
  186.5 59.9 %copy-start.10 = (bf16[1024,512]{1,0:T(8,128)(2,1)}, bf16[1024,512]{1,0:T(8,128)(2,1)S(1)}, u32[]{:S(2)}) copy-start(bf16[1024,512]{1,0:T(8,128)(2,1)S(1)} %collective-permute-done.21.refs_11_.refs_7_) | copy-start | bytes 3145732
  186.5 48.6 %copy-start.7 = (bf16[1024,512]{1,0:T(8,128)(2,1)}, bf16[1024,512]{1,0:T(8,128)(2,1)S(1)}, u32[]{:S(2)}) copy-start(bf16[1024,512]{1,0:T(8,128)(2,1)S(1)} %collective-permute-done.22.refs_6_.refs_8_) | copy-start | bytes 3145732
  186.5 48.6 %collective-permute-start.23 = (bf16[1024,512]{1,0:T(8,128)(2,1)S(1)}, bf16[1024,512]{1,0:T(8,128)(2,1)S(1)}, u32[]{:S(2)}, u32[]{:S(2)}) collective-permute-start(bf16[1024,512]{1,0:T(8,128)(2,1)S(1)} %collective-permute-done.21.refs_11_.refs_7_), channel_id=1, source_target_pairs={{0,1},{1,2},{2,3},{3,0},{4,5},{5,6},{6,7},{7,4},{8,11},{9,8},{10,9... | collective-permute-start | bytes 3145736 | tf_op jit(solution)/shard_map/ppermute | solution.py:45
  187.1 56.4 %collective-permute-start.26 = (bf16[1024,512]{1,0:T(8,128)(2,1)S(1)}, bf16[1024,512]{1,0:T(8,128)(2,1)S(1)}, u32[]{:S(2)}, u32[]{:S(2)}) collective-permute-start(bf16[1024,512]{1,0:T(8,128)(2,1)S(1)} %constant_dynamic-update-slice_fusion.refs_9_.refs_5_), channel_id=1, source_target_pairs={{0,1},{1,2},{2,3},{3,0},{4,5},{5,6},{6,7},{7,4},{8,11},{9,8},{10,9... | collective-permute-start | bytes 3145736 | tf_op jit(solution)/shard_map/ppermute | solution.py:45
  242.8 3.6 %collective-permute-start.24 = (f32[512,640]{1,0:T(8,128)}, f32[512,640]{1,0:T(8,128)S(1)}, u32[]{:S(2)}, u32[]{:S(2)}) collective-permute-start(f32[512,640]{1,0:T(8,128)} %project_first.1.refs_3_), channel_id=1, source_target_pairs={{0,8},{1,9},{2,10},{3,11},{4,12},{5,13},{6,14},{7,15},{8,0},{9,1},... | collective-permute-start | bytes 3932168 | tf_op jit(solution)/shard_map/ppermute | solution.py:45
  243.5 15.8 %copy-start.9 = (bf16[1024,512]{1,0:T(8,128)(2,1)}, bf16[1024,512]{1,0:T(8,128)(2,1)S(1)}, u32[]{:S(2)}) copy-start(bf16[1024,512]{1,0:T(8,128)(2,1)S(1)} %collective-permute-done.26.refs_10_.refs_6_) | copy-start | bytes 3145732
  243.5 16.2 %collective-permute-start.28 = (bf16[1024,512]{1,0:T(8,128)(2,1)S(1)}, bf16[1024,512]{1,0:T(8,128)(2,1)S(1)}, u32[]{:S(2)}, u32[]{:S(2)}) collective-permute-start(bf16[1024,512]{1,0:T(8,128)(2,1)S(1)} %collective-permute-done.26.refs_10_.refs_6_), channel_id=1, source_target_pairs={{0,1},{1,2},{2,3},{3,0},{4,5},{5,6},{6,7},{7,4},{8,11},{9,8},{10,9... | collective-permute-start | bytes 3145736 | tf_op jit(solution)/shard_map/ppermute | solution.py:45
  259.3 3.3 %collective-permute-start.25 = (f32[512,640]{1,0:T(8,128)}, f32[512,640]{1,0:T(8,128)S(1)}, u32[]{:S(2)}, u32[]{:S(2)}) collective-permute-start(f32[512,640]{1,0:T(8,128)} %get-tuple-element.73.refs_3_), channel_id=1, source_target_pairs={{0,8},{1,9},{2,10},{3,11},{4,12},{5,13},{6,14},{7,15},{8,0},{9,1},... | collective-permute-start | bytes 3932168 | tf_op jit(solution)/shard_map/ppermute | solution.py:45
  259.8 15.7 %collective-permute-start.29 = (bf16[1024,512]{1,0:T(8,128)(2,1)S(1)}, bf16[1024,512]{1,0:T(8,128)(2,1)S(1)}, u32[]{:S(2)}, u32[]{:S(2)}) collective-permute-start(bf16[1024,512]{1,0:T(8,128)(2,1)S(1)} %collective-permute-done.28.refs_11_.refs_7_), channel_id=1, source_target_pairs={{0,1},{1,2},{2,3},{3,0},{4,5},{5,6},{6,7},{7,4},{8,11},{9,8},{10,9... | collective-permute-start | bytes 3145736 | tf_op jit(solution)/shard_map/ppermute | solution.py:45
  281.1 3.6 %collective-permute-start.30 = (f32[512,640]{1,0:T(8,128)}, f32[512,640]{1,0:T(8,128)S(1)}, u32[]{:S(2)}, u32[]{:S(2)}) collective-permute-start(f32[512,640]{1,0:T(8,128)} %third_rest.1.refs_3_), channel_id=1, source_target_pairs={{0,8},{1,9},{2,10},{3,11},{4,12},{5,13},{6,14},{7,15},{8,0},{9,1},... | collective-permute-start | bytes 3932168 | tf_op jit(solution)/shard_map/ppermute | solution.py:45
  296.4 5.4 %collective-permute-start.31 = (bf16[256,4096]{1,0:T(8,128)(2,1)}, bf16[256,4096]{1,0:T(8,128)(2,1)S(1)}, u32[]{:S(2)}, u32[]{:S(2)}) collective-permute-start(bf16[256,4096]{1,0:T(8,128)(2,1)} %get-tuple-element.82), channel_id=1, source_target_pairs={{0,8},{1,9},{2,10},{3,11},{4,12},{5,13},{6,14},{7,15},{8,0},{9,1},... | collective-permute-start | bytes 6291464 | tf_op jit(solution)/shard_map/ppermute | solution.py:45
  296.8 5.0 %collective-permute-start.32 = (f32[256,640]{1,0:T(8,128)}, f32[256,640]{1,0:T(8,128)S(1)}, u32[]{:S(2)}, u32[]{:S(2)}) collective-permute-start(f32[256,640]{1,0:T(8,128)} %get-tuple-element.83.mine), channel_id=1, source_target_pairs={{0,8},{1,9},{2,10},{3,11},{4,12},{5,13},{6,14},{7,15},{8,0},{9,1},... | collective-permute-start | bytes 1966088 | tf_op jit(solution)/shard_map/ppermute | solution.py:45
  (14 other events, 41.4 us)

commit v2 on v1

--- a/solution.py
+++ b/solution.py
@@ -59,6 +59,24 @@
 
 def to_chip(value, steps):
     return shift(value, lambda chip, core, xlo, z: (chip + steps, core, xlo, z))
+
+
+def to_next_pair(value):
+    def move(chip, core, xlo, z):
+        return chip + 1, core, xlo + (chip % 4 == 3), z
+
+    return shift(value, move)
+
+
+def to_next(value, hop):
+    def move(chip, core, xlo, z):
+        xhi, y = divmod(chip, 4)
+        start = (y - hop + 2 * hop * core) % 4
+        if start >= 2 and hop == ((start + core) % 2):
+            xhi = 1 - xhi
+        return xhi * 4 + (y + 1 - 2 * core) % 4, core, xlo, z
+
+    return shift(value, move)
 
 
 def adamw_update(master, moment, second, gradient):
@@ -168,17 +186,25 @@
         self.lower.wait()
 
 
-def chunks_of(pieces):
-    return [
-        piece.at[pl.ds(start, SUB)] for piece in pieces for start in range(0, piece.shape[0], SUB)
-    ]
-
-
-def read_pieces(pieces, slots, sems):
+def chunks_of(pieces, flip):
+    for piece in pieces:
+        for start in range(0, piece.shape[0], SUB):
+            if flip is not None and piece.shape[0] == 2 * SUB:
+                start = pl.multiple_of(start + flip * (SUB - 2 * start), SUB)
+            yield piece.at[pl.ds(start, SUB)]
+
+
+def read_pieces(pieces, slots, sems, flip=None):
     return [
         pltpu.make_async_copy(chunk, slots.at[index], sems.at[index])
-        for index, chunk in enumerate(chunks_of(pieces))
+        for index, chunk in enumerate(chunks_of(pieces, flip))
     ]
+
+
+def projected_of(mine, theirs):
+    summed = mine[...] + theirs[...]
+    scale = lax.rsqrt(summed[:, KVW : KVW + 1] * (1.0 / D) + norm_eps)
+    return (summed[:, :KVW] * scale).astype(jnp.bfloat16)
 
 
 def layer_kernel(plan, *refs):
@@ -190,13 +216,13 @@
 
     (table,) = take(1)
     blocks = take(plan.blocks + plan.picks)
-    mine, theirs = take(2) if plan.last else (None, None)
+    mine = take(plan.blocks if plan.last else 0)
+    theirs = take(plan.blocks if plan.last else 0)
     last = take(plan.last)
-    begun = take(1) if plan.adds else []
     after = take(plan.after)
     fresh = take(plan.blocks) if plan.last else []
     kept = take(1) if plan.keeps else []
-    out = take(1) if plan.after else []
+    out = take(plan.blocks - plan.skip if plan.after else 0)
     columns, column_sems = take(2)
     last_slots, last_sems = take(2) if plan.last else (None, None)
     after_slots, after_sems = take(2) if plan.after else (None, None)
@@ -207,8 +233,9 @@
     chunks = range(8) if plan.last else taken_up
     read = picked_columns if plan.picks else read_columns
     reads = read(table, blocks, columns, column_sems, chunks)
-    last_reads = read_pieces(last, last_slots, last_sems) if plan.last else []
-    after_reads = read_pieces(after, after_slots, after_sems) if plan.after else []
+    flips = [None if at is None else table[at] for at in (plan.last_flip, plan.after_flip)]
+    last_reads = read_pieces(last, last_slots, last_sems, flips[0]) if plan.last else []
+    after_reads = read_pieces(after, after_slots, after_sems, flips[1]) if plan.after else []
 
     def begin(chunk):
         if chunk not in chunks:
@@ -224,16 +251,13 @@
         begin(chunks[0] + ahead)
     rows = plan.blocks * ROWS
     if plan.last:
-        summed = mine[...] + theirs[...]
-        scale = lax.rsqrt(summed[:, KVW : KVW + 1] * (1.0 / D) + norm_eps)
-        projected = (summed[:, :KVW] * scale).astype(jnp.bfloat16)
+        projected = jnp.concatenate(
+            [projected_of(here, there) for here, there in zip(mine, theirs)], axis=0
+        )
     skip = plan.skip * ROWS
     if plan.after:
         total = jnp.zeros((rows - skip, KVW), jnp.float32)
         squares = jnp.zeros((rows - skip, 1), jnp.float32)
-        if plan.adds:
-            total += begun[0][:, :KVW]
-            squares += begun[0][:, KVW : KVW + 1]
     stores = []
     for chunk in chunks:
         begin(chunk + AHEAD)
@@ -285,8 +309,10 @@
             flat = part.astype(jnp.float32)
             squares += jnp.sum(flat * flat, axis=1, keepdims=True)
     if plan.after:
-        out[0][:, :KVW] = total
-        out[0][:, KVW:] = jnp.broadcast_to(squares, (rows - skip, LANES))
+        for index, product in enumerate(out):
+            part = slice(index * ROWS, (index + 1) * ROWS)
+            product[:, :KVW] = total[part]
+            product[:, KVW:] = jnp.broadcast_to(squares[part], (ROWS, LANES))
     for store in stores:
         store.wait()
 
@@ -298,17 +324,19 @@
     after: int
     first: int = 0
     count: int = 0
-    adds: bool = False
     skip: int = 0
     swaps: bool = False
     keeps: bool = False
+    last_flip: int | None = None
+    after_flip: int | None = None
     picks: bool = False
 
 
-def layer_call(table, blocks, sums=(), last=(), begun=(), after=(), name="layer", **plan):
+def layer_call(table, blocks, products=(), last=(), after=(), name="layer", **plan):
     count = sum(piece.shape[0] for piece in after) // SUB
     picks = plan.get("picks", False)
-    plan = Plan(len(blocks) - picks, len(last), len(after), count=count, adds=len(begun) > 0, **plan)
+    plan = Plan(len(blocks) - picks, len(last), len(after), count=count, **plan)
+    sums = (*products, *map(to_core, products))
     rows = plan.blocks * ROWS
     any_space = pl.BlockSpec(memory_space=pl.ANY)
     vmem = pl.BlockSpec(memory_space=pltpu.VMEM)
@@ -325,8 +353,9 @@
         out_shape.append(jax.ShapeDtypeStruct((HALF, KVW), jnp.bfloat16))
         out_specs.append(any_space)
     if plan.after:
-        out_shape.append(jax.ShapeDtypeStruct((rows - plan.skip * ROWS, KVW + LANES), jnp.float32))
-        out_specs.append(vmem)
+        ahead = plan.blocks - plan.skip
+        out_shape += [jax.ShapeDtypeStruct((ROWS, KVW + LANES), jnp.float32)] * ahead
+        out_specs += [vmem] * ahead
         scratch += [
             pltpu.VMEM((plan.count, SUB, KVW), jnp.bfloat16),
             pltpu.SemaphoreType.DMA((plan.count,)),
@@ -341,7 +370,6 @@
         + [any_space] * len(blocks)
         + [vmem] * len(sums)
         + [any_space] * len(last)
-        + [vmem] * len(begun)
         + [any_space] * len(after),
         out_specs=out_specs,
         out_shape=out_shape,
@@ -349,7 +377,7 @@
         compiler_params=pltpu.CompilerParams(vmem_limit_bytes=VMEM),
         cost_estimate=COST,
         name=name,
-    )(table, *blocks, *sums, *last, *begun, *after)
+    )(table, *blocks, *sums, *last, *after)
 
 
 def final_kernel(table, keep, got, mine, theirs, *refs):
@@ -380,9 +408,7 @@
 
     for ahead in range(2 * AHEAD):
         begin(ahead)
-    summed = mine[...] + theirs[...]
-    scale = lax.rsqrt(summed[:, KVW : KVW + 1] * (1.0 / D) + norm_eps)
-    projected = (summed[:, :KVW] * scale).astype(jnp.bfloat16)
+    projected = projected_of(mine, theirs)
     for chunk in range(16):
         begin(chunk + 2 * AHEAD)
         reads[chunk].wait()
@@ -445,8 +471,11 @@
         owner = lax.rem(z + jnp.where(is_upper, step, 4 - step), 4)
         return jnp.stack([owner + 4 * xlo, owner + 4 * (1 - xlo)], axis=1).reshape(8) * SUB
 
-    filler = jnp.zeros((7,), jnp.int32)
-    table = jnp.concatenate([columns(upper), core_word, filler, columns(~upper)]).astype(jnp.int32)
+    y = lax.rem(lax.div(lax.axis_index("section"), 2), 4)
+    flips = jnp.stack([y < 2, y == 0]).astype(jnp.int32)
+    filler = jnp.zeros((5,), jnp.int32)
+    table = jnp.concatenate([columns(upper), core_word, flips, filler, columns(~upper)])
+    table = table.astype(jnp.int32)
 
     states, mine, theirs, keep, give = update_call(
         core_word,
@@ -461,91 +490,89 @@
     odd_rows = jnp.where(upper, mine, other)
     got = to_core(after(give, other))
 
-    home_own = [even_rows, to_ring(even_rows)]
+    queue = []
+
+    def ring(value, *events):
+        value = to_ring(after(value, *queue[-3:-1], *events))
+        queue.append(value)
+        return value
+
+    home_own = [even_rows, ring(even_rows)]
     home_other = to_pair(even_rows)
-    near_odd = to_chip(odd_rows, 1)
-
-    phase = (home_own[1], home_other, near_odd)
-    home_own.append(to_ring(after(home_own[1], *phase)))
-    home_others = [after(home_other, *phase)]
-    home_others.append(to_ring(home_others[0]))
-    near_odd = after(near_odd, *phase)
-    far = to_chip(near_odd, 1)
+    near_odd = to_next_pair(odd_rows)
+
+    home_own.append(ring(home_own[1], near_odd))
+    near_odd = after(near_odd, home_own[1])
+    far = to_next_pair(near_odd)
     third_other = to_pair(near_odd)
+    home_others = [home_other, ring(home_other)]
     odd = jnp.where(upper, keep, got)
 
-    phase = (home_own[2], home_others[1], far, third_other, odd)
-    home_own.append(to_ring(after(home_own[2], *phase)))
-    home_others.append(to_ring(after(home_others[1], *phase)))
-    far = after(far, *phase)
-    far_other = to_pair(far)
-    near_even = to_chip(after(even_rows, *phase), 1)
-    odd = to_chip(after(odd, *phase), 2)
-
-    phase = (home_own[3], home_others[2], far_other, near_even)
-    home_others.append(to_ring(after(home_others[2], *phase)))
-    first = [after(together(far, far_other), *phase)]
-    first.append(to_ring(first[0]))
-    near_even = after(near_even, *phase)
-    second_other = to_pair(near_even)
-    third = [together(near_odd, third_other)]
+    home_own.append(ring(home_own[2]))
+    near_even = to_next_pair(after(even_rows, home_own[2]))
+    home_others.append(ring(home_others[1], odd))
+    far_other = to_pair(after(far, home_others[1]))
+    odd = to_next(after(odd, far, home_others[1]), 0)
+    first = [together(after(far, home_own[3]), far_other)]
+    first.append(ring(first[0], third_other))
+    second_other = to_pair(after(near_even, home_others[2]))
+    home_others.append(ring(home_others[2], near_even))
 
     home = [piece for pair in zip(home_own, home_others) for piece in pair]
     (product,) = layer_call(table, (keep, got), after=home, picks=True, name="project_home")
-    phase = (first[1], home_others[3], second_other)
-    first.append(to_ring(after(first[1], *phase)))
-    second = [after(together(near_even, second_other), *phase)]
-    second.append(to_ring(second[0]))
+    first.append(ring(first[1]))
+    second = [together(after(near_even, first[1]), second_other)]
+    third = [together(after(near_odd, first[1]), third_other)]
+    second.append(ring(second[0], odd, third[0]))
+    odd = to_next(after(odd, first[1]), 1)
     even, home_here = layer_call(
         table,
         (keep, got),
-        sums=(product, to_core(after(product, *phase))),
+        products=(product,),
         last=home,
         picks=True,
         keeps=True,
         name="expand_home",
     )
-    phase = (first[2], second[1], odd, even, third[0])
-    even = to_chip(even, 2)
-    home_there = to_core(after(home_here, *phase))
-    first.append(to_ring(after(first[2], *phase)))
-    second.append(to_ring(after(second[1], *phase)))
-
-    phase = (first[3], second[2])
-    second.append(to_ring(after(second[2], *phase)))
-    third.append(to_ring(after(third[0], *phase)))
-
-    even = after(even, second[3])
-    phase = (second[3], third[1], home_there)
-    third.append(to_ring(after(third[1], *phase)))
-    third.append(to_ring(third[2]))
-
-    (product,) = layer_call(table, (even, odd), after=first, name="project_first")
-    even, odd, product = layer_call(
+    first.append(ring(first[2], even))
+    even = to_next(even, 0)
+    third.append(ring(third[0]))
+    second.append(ring(second[1], odd))
+    third.append(ring(third[1], even))
+    even = to_next(after(even, third[1]), 1)
+    home_there = to_core(after(home_here, second[2]))
+    second.append(ring(second[2]))
+    third.append(ring(third[2]))
+
+    even = after(even, third[2])
+    products = layer_call(table, (even, odd), after=first, after_flip=9, name="project_first")
+    even, odd, *products = layer_call(
         table,
         (even, odd),
-        sums=(product, to_core(product)),
+        products=products,
         last=first,
         after=second,
+        last_flip=9,
+        after_flip=10,
         name="first_second",
     )
-    even, odd, product = layer_call(
+    even, odd, *products = layer_call(
         table,
         (even, odd),
-        sums=(product, to_core(product)),
+        products=products,
         last=second,
-        after=third[:3],
+        after=third,
+        last_flip=10,
+        after_flip=10,
         name="second_third",
-    )
-    (product,) = layer_call(
-        table, (even, odd), begun=(product,), after=third[3:], first=6, name="third_rest"
     )
     keep, give, product = layer_call(
         table,
         (even, odd),
-        sums=(product, to_core(product)),
+        products=products,
         last=third,
         after=[home_here],
+        last_flip=10,
         skip=1,
         swaps=True,
         name="third_home",

time: 313 us -> 310 us (level); the launches traced: 313 us -> 305 us
  starting transfers between devices: 81.2 us -> 69.4 us
  waiting for transfers between devices: 139 us -> 150 us
  Pallas kernels: 78.3 us -> 73.5 us
    ppermute x33 -> x38, starting transfers between devices: 81.2 us -> 69.4 us  [shift(): return lax.ppermute(value, AXES, pairs)]
    ppermute x33 -> x38, waiting for transfers between devices: 139 us -> 150 us  [shift(): return lax.ppermute(value, AXES, pairs)]
    pallas_call x7 -> x6, Pallas kernels: 57.8 us -> 53 us  [layer_call(): pl.pallas_call(functools.partial(layer_kernel, plan), in_specs=[pl.BlockS...]
    unnamed x59 -> x61, local copies, waits for them, and re-layouts: 7.98 us -> 7.48 us
  transfers between devices with their start and end apart: 33 -> 38, of which waited for: 18 -> 21; matrix products, arithmetic and copies ran while one was open for 2% -> 1% of each run, Pallas kernels for 14% -> 17%
where the time goes in v2:
time: 310 us; the launch traced here: 305 us
  waiting for transfers between devices  150 us (48%)
  Pallas kernels  73.5 us (24%)
  starting transfers between devices  69.4 us (22%)
  local copies, waits for them, and re-layouts  8.44 us (3%)
    ppermute x38, waiting for transfers between devices, shift(): return lax.ppermute(value, AXES, pairs)  150 us
    ppermute x38, starting transfers between devices, shift(): return lax.ppermute(value, AXES, pairs)  69.4 us
    pallas_call x6, Pallas kernels, layer_call(): pl.pallas_call(functools.partial(layer_kernel, plan), in_specs=[pl.BlockS...  53 us
    pallas_call x1, Pallas kernels, update_call(): pl.pallas_call(update_kernel, grid_spec=pltpu.PrefetchScalarGridSpec(num_...  11.4 us
    pallas_call x1, Pallas kernels, final_call(): pl.pallas_call(final_kernel, in_specs=[pl.BlockSpec(memory_space=pltpu.SM...  9.02 us
    unnamed x61, local copies, waits for them, and re-layouts  7.48 us
  transfers between devices with their start and end apart: 38, of which 21 were waited for; matrix products, arithmetic and copies ran while one was open for 1% of the time, Pallas kernels for 17%

profile of v2, /device:TPU:1, one launch (start us, length us, event | category | flops | bytes accessed | tf_op | source)
XLA Modules:
  0.0 304.9 jit_solution(3052852787391968659)
XLA Ops:
  0.6 11.4 %update.1 = (f32[2,512,512]{2,1,0:T(8,128)}, f32[2,512,512]{2,1,0:T(8,128)}, f32[2,512,512]{2,1,0:T(8,128)}, bf16[512,512]{1,0:T(8,128)(2,1)}, bf16[512,512]{1,0...) custom-call(s32[1]{0:T(128)} %bitcast.core_ref, f32[2,512,512]{2,1,0:T(8,128)} %bitcast.14, ...), custom_call_target="tpu_custom_call" | custom-call | flops 1 | bytes 1 | tf_op jit(solution)/shard_map/update/pallas_call | solution.py:130
  12.0 1.5 collective-permute-start
  13.5 1.7 collective-permute-done
  15.7 1.1 broadcast_select_fusion.1
  16.8 1.4 collective-permute-start.2
  18.2 3.8 %collective-permute-start.3 = (bf16[512,512]{1,0:T(8,128)(2,1)S(1)}, bf16[512,512]{1,0:T(8,128)(2,1)S(1)}, u32[]{:S(2)}, u32[]{:S(2)}) collective-permute-start(bf16[512,512]{1,0:T(8,128)(2,1)S(1)} %get-tuple-element.65.refs_3_.refs_5_), channel_id=1, source_target_pairs={{0,1},{1,2},{2,3},{3,0},{4,5},{5,6},{6,7},{7,4},{8,11},{9,8},{10,9... | collective-permute-start | bytes 1572872 | tf_op jit(solution)/shard_map/ppermute | solution.py:45
  21.9 1.3 collective-permute-start.5
  23.2 7.0 %collective-permute-done.2.refs_4_.refs_6_ = bf16[512,512]{1,0:T(8,128)(2,1)S(1)} collective-permute-done((bf16[512,512]{1,0:T(8,128)(2,1)S(1)}, bf16[512,512]{1,0:T(8,128)(2,1)S(1)}, u32[]{:S(2)}, u32[]{:S(2)}) %collective-permute-start.2) | collective-permute-done | bytes 524320 | tf_op jit(solution)/shard_map/ppermute | solution.py:45
  30.3 7.7 %collective-permute-done.5 = bf16[512,512]{1,0:T(8,128)(2,1)S(1)} collective-permute-done((bf16[512,512]{1,0:T(8,128)(2,1)S(1)}, bf16[512,512]{1,0:T(8,128)(2,1)S(1)}, u32[]{:S(2)}, u32[]{:S(2)}) %collective-permute-start.5) | collective-permute-done | bytes 524320 | tf_op jit(solution)/shard_map/ppermute | solution.py:45
  38.6 7.7 %collective-permute-done.6.refs_7_.refs_9_ = bf16[512,512]{1,0:T(8,128)(2,1)S(1)} collective-permute-done((bf16[512,512]{1,0:T(8,128)(2,1)S(1)}, bf16[512,512]{1,0:T(8,128)(2,1)S(1)}, u32[]{:S(2)}, u32[]{:S(2)}) %collective-permute-start.6) | collective-permute-done | bytes 524320 | tf_op jit(solution)/shard_map/ppermute | solution.py:45
  46.3 1.8 collective-permute-start.8
  48.1 3.9 %collective-permute-done.4.refs_6_.refs_8_ = bf16[512,512]{1,0:T(8,128)(2,1)} collective-permute-done((bf16[512,512]{1,0:T(8,128)(2,1)S(1)}, bf16[512,512]{1,0:T(8,128)(2,1)}, u32[]{:S(2)}, u32[]{:S(2)}) %collective-permute-start.4) | collective-permute-done | bytes 524320 | tf_op jit(solution)/shard_map/ppermute | solution.py:45
  52.0 2.3 collective-permute-done.13
  54.3 1.5 broadcast_select_fusion
  55.9 1.5 collective-permute-start.15
  57.4 1.4 collective-permute-start.9
  59.1 6.7 %collective-permute-done.14 = bf16[512,512]{1,0:T(8,128)(2,1)S(1)} collective-permute-done((bf16[512,512]{1,0:T(8,128)(2,1)S(1)}, bf16[512,512]{1,0:T(8,128)(2,1)S(1)}, u32[]{:S(2)}, u32[]{:S(2)}) %collective-permute-start.14) | collective-permute-done | bytes 524320 | tf_op jit(solution)/shard_map/ppermute | solution.py:45
  65.9 11.2 %collective-permute-done.15 = bf16[512,512]{1,0:T(8,128)(2,1)S(1)} collective-permute-done((bf16[512,512]{1,0:T(8,128)(2,1)S(1)}, bf16[512,512]{1,0:T(8,128)(2,1)S(1)}, u32[]{:S(2)}, u32[]{:S(2)}) %collective-permute-start.15) | collective-permute-done | bytes 524320 | tf_op jit(solution)/shard_map/ppermute | solution.py:45
  77.1 1.5 collective-permute-done.9
  78.6 1.7 collective-permute-start.10
  81.5 15.2 %collective-permute-done.10.refs_10_.refs_12_ = bf16[512,512]{1,0:T(8,128)(2,1)S(1)} collective-permute-done((bf16[512,512]{1,0:T(8,128)(2,1)S(1)}, bf16[512,512]{1,0:T(8,128)(2,1)S(1)}, u32[]{:S(2)}, u32[]{:S(2)}) %collective-permute-start.10) | collective-permute-done | bytes 524320 | tf_op jit(solution)/shard_map/ppermute | solution.py:45
  97.4 5.2 %project_home.1.refs_3_ = f32[256,640]{1,0:T(8,128)} custom-call(s32[24]{0:T(128)} %concatenate.12.refs_0_.table, bf16[256,4096]{1,0:T(8,128)(2,1)} %get-tuple-element.56.refs_1_, bf16[256,4096]{1,0:T(8,128)(2,1)} %collective-permute-done.1.refs_2_, bf16[512,512]{1,0:T(8,128)(2,1)} %copy-done.6, bf16[512,512]{1,0:T(8,128)(2,1)} %copy-done.12, ...), custom_call_target="tpu_custom_call" | custom-call | flops 1 | bytes 1 | tf_op jit(solution)/shard_map/project_home/pallas_call | solution.py:367
  102.6 11.5 %collective-permute-start.11 = (f32[256,640]{1,0:T(8,128)}, f32[256,640]{1,0:T(8,128)S(1)}, u32[]{:S(2)}, u32[]{:S(2)}) collective-permute-start(f32[256,640]{1,0:T(8,128)} %project_home.1.refs_3_), channel_id=1, source_target_pairs={{0,8},{1,9},{2,10},{3,11},{4,12},{5,13},{6,14},{7,15},{8,0},{9,1},... | collective-permute-start | bytes 1966088 | tf_op jit(solution)/shard_map/ppermute | solution.py:45
  114.4 13.3 %collective-permute-done.18 = bf16[512,512]{1,0:T(8,128)(2,1)S(1)} collective-permute-done((bf16[512,512]{1,0:T(8,128)(2,1)S(1)}, bf16[512,512]{1,0:T(8,128)(2,1)S(1)}, u32[]{:S(2)}, u32[]{:S(2)}) %collective-permute-start.18) | collective-permute-done | bytes 524320 | tf_op jit(solution)/shard_map/ppermute | solution.py:45
  127.9 0.9 copy-done.19
  128.8 7.3 %expand_home.1 = (bf16[256,4096]{1,0:T(8,128)(2,1)}, bf16[4096,512]{1,0:T(8,128)(2,1)}) custom-call(s32[24]{0:T(128)} %concatenate.12.refs_0_.table, bf16[256,4096]{1,0:T(8,128)(2,1)} %get-tuple-element.56.refs_1_, bf16[256,4096]{1,0:T(8,128)(2,1)} %collective-permute-done.1.refs_2_, f32[256,640]{1,0:T(8,128)} %project_home.1.refs_3_, ...), custom_call_target="tpu_custom_call" | custom-call | flops 1 | bytes 1 | tf_op jit(solution)/shard_map/expand_home/pallas_call | solution.py:367
  136.1 12.7 %collective-permute-start.12 = (bf16[256,4096]{1,0:T(8,128)(2,1)}, bf16[256,4096]{1,0:T(8,128)(2,1)S(1)}, u32[]{:S(2)}, u32[]{:S(2)}) collective-permute-start(bf16[256,4096]{1,0:T(8,128)(2,1)} %get-tuple-element.67), channel_id=1, source_target_pairs={{0,16},{1,17},{2,18},{3,19},{4,20},{5,21},{6,22},{7,23},{8,56},{9,... | collective-permute-start | bytes 6291464 | tf_op jit(solution)/shard_map/ppermute | solution.py:45
  148.8 3.3 %collective-permute-start.25 = (bf16[256,4096]{1,0:T(8,128)(2,1)}, bf16[256,4096]{1,0:T(8,128)(2,1)S(1)}, u32[]{:S(2)}, u32[]{:S(2)}) collective-permute-start(bf16[256,4096]{1,0:T(8,128)(2,1)} %collective-permute-done.19), channel_id=1, source_target_pairs={{0,80},{1,81},{2,82},{3,83},{4,84},{5,85},{6,86},{7,87},{8,56},{9,... | collective-permute-start | bytes 6291464 | tf_op jit(solution)/shard_map/ppermute | solution.py:45
  153.4 30.7 %collective-permute-done.12 = bf16[256,4096]{1,0:T(8,128)(2,1)S(1)} collective-permute-done((bf16[256,4096]{1,0:T(8,128)(2,1)}, bf16[256,4096]{1,0:T(8,128)(2,1)S(1)}, u32[]{:S(2)}, u32[]{:S(2)}) %collective-permute-start.12) | collective-permute-done | bytes 2097184 | tf_op jit(solution)/shard_map/ppermute | solution.py:45
  184.1 10.5 %collective-permute-done.25.refs_2_ = bf16[256,4096]{1,0:T(8,128)(2,1)S(1)} collective-permute-done((bf16[256,4096]{1,0:T(8,128)(2,1)}, bf16[256,4096]{1,0:T(8,128)(2,1)S(1)}, u32[]{:S(2)}, u32[]{:S(2)}) %collective-permute-start.25) | collective-permute-done | bytes 2097184 | tf_op jit(solution)/shard_map/ppermute | solution.py:45
  194.6 1.8 collective-permute-start.28
  196.9 11.8 %collective-permute-done.28.refs_13_.refs_9_ = bf16[1024,512]{1,0:T(8,128)(2,1)} collective-permute-done((bf16[1024,512]{1,0:T(8,128)(2,1)S(1)}, bf16[1024,512]{1,0:T(8,128)(2,1)}, u32[]{:S(2)}, u32[]{:S(2)}) %collective-permute-start.28) | collective-permute-done | bytes 1048608 | tf_op jit(solution)/shard_map/ppermute | solution.py:45
  208.7 2.9 collective-permute-start.29
  211.6 2.1 collective-permute-start.37
  213.7 6.1 %collective-permute-done.24.refs_13_.refs_9_ = bf16[1024,512]{1,0:T(8,128)(2,1)S(1)} collective-permute-done((bf16[1024,512]{1,0:T(8,128)(2,1)S(1)}, bf16[1024,512]{1,0:T(8,128)(2,1)S(1)}, u32[]{:S(2)}, u32[]{:S(2)}) %collective-permute-start.24) | collective-permute-done | bytes 1048608 | tf_op jit(solution)/shard_map/ppermute | solution.py:45
  219.8 1.3 copy-done.2
  221.2 6.4 %project_first.1 = (f32[256,640]{1,0:T(8,128)}, f32[256,640]{1,0:T(8,128)}) custom-call(s32[24]{0:T(128)} %concatenate.12.refs_0_.table, bf16[256,4096]{1,0:T(8,128)(2,1)} %copy-done.2, bf16[256,4096]{1,0:T(8,128)(2,1)} %copy-done.1, bf16[1024,512]{1,0:T(8,128)(2,1)} %copy-done.4, bf16[1024,512]{1,0:T(8,128)(2,1)} %collective-permute-done.16.refs_4_.refs_8_, ...), custom_call_target="tpu_custom_call" | custom-call | flops 1 | bytes 1 | tf_op jit(solution)/shard_map/project_first/pallas_call | solution.py:367
  227.5 5.0 %collective-permute-start.26 = (f32[256,640]{1,0:T(8,128)}, f32[256,640]{1,0:T(8,128)S(1)}, u32[]{:S(2)}, u32[]{:S(2)}) collective-permute-start(f32[256,640]{1,0:T(8,128)} %get-tuple-element.84.refs_3_), channel_id=1, source_target_pairs={{0,8},{1,9},{2,10},{3,11},{4,12},{5,13},{6,14},{7,15},{8,0},{9,1},... | collective-permute-start | bytes 1966088 | tf_op jit(solution)/shard_map/ppermute | solution.py:45
  232.7 1.8 collective-permute-done.26.refs_5_
  236.2 11.8 %first_second.1 = (bf16[256,4096]{1,0:T(8,128)(2,1)}, bf16[256,4096]{1,0:T(8,128)(2,1)}, f32[256,640]{1,0:T(8,128)}, f32[256,640]{1,0:T(8,128)}) custom-call(s32[24]{0:T(128)} %concatenate.12.refs_0_.table, bf16[256,4096]{1,0:T(8,128)(2,1)} %copy-done.2, bf16[256,4096]{1,0:T(8,128)(2,1)} %copy-done.1, f32[256,640]{1,0:T(8,128)} %get-tuple-element.84.refs_3_, ...), custom_call_target="tpu_custom_call" | custom-call | flops 1 | bytes 1 | tf_op jit(solution)/shard_map/first_second/pallas_call | solution.py:367
  248.1 1.5 collective-permute-start.30
  249.6 9.6 %collective-permute-start.31 = (f32[256,640]{1,0:T(8,128)}, f32[256,640]{1,0:T(8,128)S(1)}, u32[]{:S(2)}, u32[]{:S(2)}) collective-permute-start(f32[256,640]{1,0:T(8,128)} %get-tuple-element.91.refs_4_), channel_id=1, source_target_pairs={{0,8},{1,9},{2,10},{3,11},{4,12},{5,13},{6,14},{7,15},{8,0},{9,1},... | collective-permute-start | bytes 1966088 | tf_op jit(solution)/shard_map/ppermute | solution.py:45
  259.2 1.9 collective-permute-done.31.refs_6_
  262.0 11.8 %second_third.1 = (bf16[256,4096]{1,0:T(8,128)(2,1)}, bf16[256,4096]{1,0:T(8,128)(2,1)}, f32[256,640]{1,0:T(8,128)}, f32[256,640]{1,0:T(8,128)}) custom-call(s32[24]{0:T(128)} %concatenate.12.refs_0_.table, bf16[256,4096]{1,0:T(8,128)(2,1)} %get-tuple-element.88.refs_1_, bf16[256,4096]{1,0:T(8,128)(2,1)} %get-tuple-element.89.refs_2_, ...), custom_call_target="tpu_custom_call" | custom-call | flops 1 | bytes 1 | tf_op jit(solution)/shard_map/second_third/pallas_call | solution.py:367
  274.4 1.8 collective-permute-done.33.refs_5_
  278.0 10.6 %third_home.1 = (bf16[256,4096]{1,0:T(8,128)(2,1)}, bf16[256,4096]{1,0:T(8,128)(2,1)}, f32[256,640]{1,0:T(8,128)}) custom-call(s32[24]{0:T(128)} %concatenate.12.refs_0_.table, bf16[256,4096]{1,0:T(8,128)(2,1)} %get-tuple-element.93.refs_1_, bf16[256,4096]{1,0:T(8,128)(2,1)} %get-tuple-element.94.refs_2_, f32[256,640]{1,0:T(8,128)} %get-tuple-element.95.refs_3_, ...), custom_call_target="tpu_custom_call" | custom-call | flops 1 | bytes 1 | tf_op jit(solution)/shard_map/third_home/pallas_call | solution.py:367
  289.2 4.8 %collective-permute-done.36.theirs = f32[256,640]{1,0:T(8,128)S(1)} collective-permute-done((f32[256,640]{1,0:T(8,128)}, f32[256,640]{1,0:T(8,128)S(1)}, u32[]{:S(2)}, u32[]{:S(2)}) %collective-permute-start.36) | collective-permute-done | bytes 655392 | tf_op jit(solution)/shard_map/ppermute | solution.py:45
  295.7 9.0 %final_layer.1 = bf16[256,8192]{1,0:T(8,128)(2,1)} custom-call(s32[24]{0:T(128)} %concatenate.12.refs_0_.table, bf16[256,4096]{1,0:T(8,128)(2,1)} %get-tuple-element.98.keep, bf16[256,4096]{1,0:T(8,128)(2,1)} %copy-done.18, f32[256,640]{1,0:T(8,128)} %get-tuple-element.100.mine, f32[256,640]{1,0:T(8,128)} %copy-done.26, ...), custom_call_target="tpu_custom_call" | custom-call | flops 1 | bytes 1 | tf_op jit(solution)/shard_map/final_layer/pallas_call | solution.py:435
  (111 shorter events, 12.9 us)
Async XLA Ops:
  12.0 42.3 %copy-start = (bf16[256,4096]{1,0:T(8,128)(2,1)S(1)}, bf16[256,4096]{1,0:T(8,128)(2,1)}, u32[]{:S(2)}) copy-start(bf16[256,4096]{1,0:T(8,128)(2,1)} %get-tuple-element.56.refs_1_) | copy-start | bytes 6291460
  12.0 3.2 %collective-permute-start = (bf16[512,512]{1,0:T(8,128)(2,1)}, bf16[512,512]{1,0:T(8,128)(2,1)S(1)}, u32[]{:S(2)}, u32[]{:S(2)}) collective-permute-start(bf16[512,512]{1,0:T(8,128)(2,1)} %get-tuple-element.58), channel_id=1, source_target_pairs={{0,8},{1,9},{2,10},{3,11},{4,12},{5,13},{6,14},{7,15},{8,0},{9,1},... | collective-permute-start | bytes 1572872 | tf_op jit(solution)/shard_map/ppermute | solution.py:45
  15.3 39.0 %collective-permute-start.1 = (bf16[256,4096]{1,0:T(8,128)(2,1)}, bf16[256,4096]{1,0:T(8,128)(2,1)}, u32[]{:S(2)}, u32[]{:S(2)}) collective-permute-start(bf16[256,4096]{1,0:T(8,128)(2,1)} %get-tuple-element.59), channel_id=1, source_target_pairs={{0,8},{1,9},{2,10},{3,11},{4,12},{5,13},{6,14},{7,15},{8,0},{9,1},... | collective-permute-start | bytes 6291464 | tf_op jit(solution)/shard_map/ppermute | solution.py:45
  16.8 40.6 %copy-start.6 = (bf16[512,512]{1,0:T(8,128)(2,1)}, bf16[512,512]{1,0:T(8,128)(2,1)S(1)}, u32[]{:S(2)}) copy-start(bf16[512,512]{1,0:T(8,128)(2,1)S(1)} %get-tuple-element.65.refs_3_.refs_5_) | copy-start | bytes 1572868
  16.8 13.5 %collective-permute-start.2 = (bf16[512,512]{1,0:T(8,128)(2,1)S(1)}, bf16[512,512]{1,0:T(8,128)(2,1)S(1)}, u32[]{:S(2)}, u32[]{:S(2)}) collective-permute-start(bf16[512,512]{1,0:T(8,128)(2,1)S(1)} %get-tuple-element.65.refs_3_.refs_5_), channel_id=1, source_target_pairs={{0,4},{1,5},{2,6},{3,7},{4,0},{5,1},{6,2},{7,3},{8,12},{9,13},{10,... | collective-permute-start | bytes 1572872 | tf_op jit(solution)/shard_map/ppermute | solution.py:45
  18.2 12.1 %collective-permute-start.3 = (bf16[512,512]{1,0:T(8,128)(2,1)S(1)}, bf16[512,512]{1,0:T(8,128)(2,1)S(1)}, u32[]{:S(2)}, u32[]{:S(2)}) collective-permute-start(bf16[512,512]{1,0:T(8,128)(2,1)S(1)} %get-tuple-element.65.refs_3_.refs_5_), channel_id=1, source_target_pairs={{0,1},{1,2},{2,3},{3,0},{4,5},{5,6},{6,7},{7,4},{8,11},{9,8},{10,9... | collective-permute-start | bytes 1572872 | tf_op jit(solution)/shard_map/ppermute | solution.py:45
  21.9 16.0 %collective-permute-start.5 = (bf16[512,512]{1,0:T(8,128)(2,1)S(1)}, bf16[512,512]{1,0:T(8,128)(2,1)S(1)}, u32[]{:S(2)}, u32[]{:S(2)}) collective-permute-start(bf16[512,512]{1,0:T(8,128)(2,1)S(1)} %get-tuple-element.102), channel_id=1, source_target_pairs={{0,16},{1,17},{2,18},{3,19},{4,20},{5,21},{6,22},{7,23},{8,24},{9,... | collective-permute-start | bytes 1572872 | tf_op jit(solution)/shard_map/ppermute | solution.py:45
  30.3 25.6 %copy-start.12 = (bf16[512,512]{1,0:T(8,128)(2,1)}, bf16[512,512]{1,0:T(8,128)(2,1)S(1)}, u32[]{:S(2)}) copy-start(bf16[512,512]{1,0:T(8,128)(2,1)S(1)} %collective-permute-done.2.refs_4_.refs_6_) | copy-start | bytes 1572868
  37.9 8.3 %collective-permute-start.6 = (bf16[512,512]{1,0:T(8,128)(2,1)S(1)}, bf16[512,512]{1,0:T(8,128)(2,1)S(1)}, u32[]{:S(2)}, u32[]{:S(2)}) collective-permute-start(bf16[512,512]{1,0:T(8,128)(2,1)S(1)} %collective-permute-done.3.refs_5_.refs_7_), channel_id=1, source_target_pairs={{0,1},{1,2},{2,3},{3,0},{4,5},{5,6},{6,7},{7,4},{8,11},{9,8},{10,9... | collective-permute-start | bytes 1572872 | tf_op jit(solution)/shard_map/ppermute | solution.py:45
  38.6 13.4 %collective-permute-start.4 = (bf16[512,512]{1,0:T(8,128)(2,1)S(1)}, bf16[512,512]{1,0:T(8,128)(2,1)}, u32[]{:S(2)}, u32[]{:S(2)}) collective-permute-start(bf16[512,512]{1,0:T(8,128)(2,1)S(1)} %collective-permute-done.2.refs_4_.refs_6_), channel_id=1, source_target_pairs={{0,1},{1,2},{2,3},{3,0},{4,5},{5,6},{6,7},{7,4},{8,11},{9,8},{10,9... | collective-permute-start | bytes 1572872 | tf_op jit(solution)/shard_map/ppermute | solution.py:45
  38.6 15.7 %collective-permute-start.13 = (bf16[512,512]{1,0:T(8,128)(2,1)S(1)}, bf16[512,512]{1,0:T(8,128)(2,1)S(1)}, u32[]{:S(2)}, u32[]{:S(2)}) collective-permute-start(bf16[512,512]{1,0:T(8,128)(2,1)S(1)} %collective-permute-done.5), channel_id=1, source_target_pairs={{0,16},{1,17},{2,18},{3,19},{4,20},{5,21},{6,22},{7,23},{8,24},{9,... | collective-permute-start | bytes 1572872 | tf_op jit(solution)/shard_map/ppermute | solution.py:45
  46.3 12.5 %collective-permute-start.8 = (bf16[512,512]{1,0:T(8,128)(2,1)S(1)}, bf16[512,512]{1,0:T(8,128)(2,1)S(1)}, u32[]{:S(2)}, u32[]{:S(2)}) collective-permute-start(bf16[512,512]{1,0:T(8,128)(2,1)S(1)} %collective-permute-done.6.refs_7_.refs_9_), channel_id=1, source_target_pairs={{0,1},{1,2},{2,3},{3,0},{4,5},{5,6},{6,7},{7,4},{8,11},{9,8},{10,9... | collective-permute-start | bytes 1572872 | tf_op jit(solution)/shard_map/ppermute | solution.py:45
  54.3 11.5 %collective-permute-start.14 = (bf16[512,512]{1,0:T(8,128)(2,1)S(1)}, bf16[512,512]{1,0:T(8,128)(2,1)S(1)}, u32[]{:S(2)}, u32[]{:S(2)}) collective-permute-start(bf16[512,512]{1,0:T(8,128)(2,1)S(1)} %collective-permute-done.13), channel_id=1, source_target_pairs={{0,4},{1,5},{2,6},{3,7},{4,0},{5,1},{6,2},{7,3},{8,12},{9,13},{10,... | collective-permute-start | bytes 1572872 | tf_op jit(solution)/shard_map/ppermute | solution.py:45
  55.8 71.9 %collective-permute-start.19 = (bf16[256,4096]{1,0:T(8,128)(2,1)}, bf16[256,4096]{1,0:T(8,128)(2,1)}, u32[]{:S(2)}, u32[]{:S(2)}) collective-permute-start(bf16[256,4096]{1,0:T(8,128)(2,1)} %broadcast_select_fusion), channel_id=1, source_target_pairs={{0,16},{1,17},{2,18},{3,19},{4,20},{5,21},{6,22},{7,23},{8,56},{9,... | collective-permute-start | bytes 6291464 | tf_op jit(solution)/shard_map/ppermute | solution.py:45
  55.9 21.2 %collective-permute-start.15 = (bf16[512,512]{1,0:T(8,128)(2,1)S(1)}, bf16[512,512]{1,0:T(8,128)(2,1)S(1)}, u32[]{:S(2)}, u32[]{:S(2)}) collective-permute-start(bf16[512,512]{1,0:T(8,128)(2,1)S(1)} %collective-permute-done.5), channel_id=1, source_target_pairs={{0,4},{1,5},{2,6},{3,7},{4,0},{5,1},{6,2},{7,3},{8,12},{9,13},{10,... | collective-permute-start | bytes 1572872 | tf_op jit(solution)/shard_map/ppermute | solution.py:45
  57.4 21.2 %collective-permute-start.9 = (bf16[512,512]{1,0:T(8,128)(2,1)S(1)}, bf16[512,512]{1,0:T(8,128)(2,1)S(1)}, u32[]{:S(2)}, u32[]{:S(2)}) collective-permute-start(bf16[512,512]{1,0:T(8,128)(2,1)S(1)} %get-tuple-element.65.refs_3_.refs_5_), channel_id=1, source_target_pairs={{0,16},{1,17},{2,18},{3,19},{4,20},{5,21},{6,22},{7,23},{8,24},{9,... | collective-permute-start | bytes 1572872 | tf_op jit(solution)/shard_map/ppermute | solution.py:45
  58.8 19.8 %collective-permute-start.7 = (bf16[512,512]{1,0:T(8,128)(2,1)}, bf16[512,512]{1,0:T(8,128)(2,1)S(1)}, u32[]{:S(2)}, u32[]{:S(2)}) collective-permute-start(bf16[512,512]{1,0:T(8,128)(2,1)} %collective-permute-done.4.refs_6_.refs_8_), channel_id=1, source_target_pairs={{0,1},{1,2},{2,3},{3,0},{4,5},{5,6},{6,7},{7,4},{8,11},{9,8},{10,9... | collective-permute-start | bytes 1572872 | tf_op jit(solution)/shard_map/ppermute | solution.py:45
  65.9 36.7 %copy-start.4 = (bf16[1024,512]{1,0:T(8,128)(2,1)}, bf16[1024,512]{1,0:T(8,128)(2,1)S(1)}, u32[]{:S(2)}) copy-start(bf16[1024,512]{1,0:T(8,128)(2,1)S(1)} %constant_dynamic-update-slice_fusion.refs_3_.refs_7_) | copy-start | bytes 3145732
  77.1 37.0 %collective-permute-start.16 = (bf16[1024,512]{1,0:T(8,128)(2,1)S(1)}, bf16[1024,512]{1,0:T(8,128)(2,1)}, u32[]{:S(2)}, u32[]{:S(2)}) collective-permute-start(bf16[1024,512]{1,0:T(8,128)(2,1)S(1)} %constant_dynamic-update-slice_fusion.refs_3_.refs_7_), channel_id=1, source_target_pairs={{0,1},{1,2},{2,3},{3,0},{4,5},{5,6},{6,7},{7,4},{8,11},{9,8},{10,9... | collective-permute-start | bytes 3145736 | tf_op jit(solution)/shard_map/ppermute | solution.py:45
  78.6 18.0 %collective-permute-start.10 = (bf16[512,512]{1,0:T(8,128)(2,1)S(1)}, bf16[512,512]{1,0:T(8,128)(2,1)S(1)}, u32[]{:S(2)}, u32[]{:S(2)}) collective-permute-start(bf16[512,512]{1,0:T(8,128)(2,1)S(1)} %collective-permute-done.7.refs_8_.refs_10_), channel_id=1, source_target_pairs={{0,1},{1,2},{2,3},{3,0},{4,5},{5,6},{6,7},{7,4},{8,11},{9,8},{10,9... | collective-permute-start | bytes 1572872 | tf_op jit(solution)/shard_map/ppermute | solution.py:45
  81.5 32.6 %copy-start.28 = (bf16[512,512]{1,0:T(8,128)(2,1)S(1)}, bf16[512,512]{1,0:T(8,128)(2,1)}, u32[]{:S(2)}) copy-start(bf16[512,512]{1,0:T(8,128)(2,1)} %copy-done.27) | copy-start | bytes 1572868
  102.6 25.3 %collective-permute-start.11 = (f32[256,640]{1,0:T(8,128)}, f32[256,640]{1,0:T(8,128)S(1)}, u32[]{:S(2)}, u32[]{:S(2)}) collective-permute-start(f32[256,640]{1,0:T(8,128)} %project_home.1.refs_3_), channel_id=1, source_target_pairs={{0,8},{1,9},{2,10},{3,11},{4,12},{5,13},{6,14},{7,15},{8,0},{9,1},... | collective-permute-start | bytes 1966088 | tf_op jit(solution)/shard_map/ppermute | solution.py:45
  114.1 13.6 %collective-permute-start.18 = (bf16[512,512]{1,0:T(8,128)(2,1)S(1)}, bf16[512,512]{1,0:T(8,128)(2,1)S(1)}, u32[]{:S(2)}, u32[]{:S(2)}) collective-permute-start(bf16[512,512]{1,0:T(8,128)(2,1)S(1)} %collective-permute-done.9), channel_id=1, source_target_pairs={{0,4},{1,5},{2,6},{3,7},{4,0},{5,1},{6,2},{7,3},{8,12},{9,13},{10,... | collective-permute-start | bytes 1572872 | tf_op jit(solution)/shard_map/ppermute | solution.py:45
  114.2 37.9 %copy-start.5 = (bf16[1024,512]{1,0:T(8,128)(2,1)}, bf16[1024,512]{1,0:T(8,128)(2,1)S(1)}, u32[]{:S(2)}) copy-start(bf16[1024,512]{1,0:T(8,128)(2,1)S(1)} %constant_dynamic-update-slice_fusion.2.refs_11_.refs_7_) | copy-start | bytes 3145732
  114.2 37.9 %collective-permute-start.17 = (bf16[1024,512]{1,0:T(8,128)(2,1)}, bf16[1024,512]{1,0:T(8,128)(2,1)}, u32[]{:S(2)}, u32[]{:S(2)}) collective-permute-start(bf16[1024,512]{1,0:T(8,128)(2,1)} %collective-permute-done.16.refs_4_.refs_8_), channel_id=1, source_target_pairs={{0,1},{1,2},{2,3},{3,0},{4,5},{5,6},{6,7},{7,4},{8,11},{9,8},{10,9... | collective-permute-start | bytes 3145736 | tf_op jit(solution)/shard_map/ppermute | solution.py:45
  127.7 24.4 %collective-permute-start.20 = (bf16[1024,512]{1,0:T(8,128)(2,1)S(1)}, bf16[1024,512]{1,0:T(8,128)(2,1)S(1)}, u32[]{:S(2)}, u32[]{:S(2)}) collective-permute-start(bf16[1024,512]{1,0:T(8,128)(2,1)S(1)} %constant_dynamic-update-slice_fusion.4.refs_11_.refs_7_), channel_id=1, source_target_pairs={{0,1},{1,2},{2,3},{3,0},{4,5},{5,6},{6,7},{7,4},{8,11},{9,8},{10,9... | collective-permute-start | bytes 3145736 | tf_op jit(solution)/shard_map/ppermute | solution.py:45
  136.1 47.9 %collective-permute-start.12 = (bf16[256,4096]{1,0:T(8,128)(2,1)}, bf16[256,4096]{1,0:T(8,128)(2,1)S(1)}, u32[]{:S(2)}, u32[]{:S(2)}) collective-permute-start(bf16[256,4096]{1,0:T(8,128)(2,1)} %get-tuple-element.67), channel_id=1, source_target_pairs={{0,16},{1,17},{2,18},{3,19},{4,20},{5,21},{6,22},{7,23},{8,56},{9,... | collective-permute-start | bytes 6291464 | tf_op jit(solution)/shard_map/ppermute | solution.py:45
  148.8 45.8 %collective-permute-start.25 = (bf16[256,4096]{1,0:T(8,128)(2,1)}, bf16[256,4096]{1,0:T(8,128)(2,1)S(1)}, u32[]{:S(2)}, u32[]{:S(2)}) collective-permute-start(bf16[256,4096]{1,0:T(8,128)(2,1)} %collective-permute-done.19), channel_id=1, source_target_pairs={{0,80},{1,81},{2,82},{3,83},{4,84},{5,85},{6,86},{7,87},{8,56},{9,... | collective-permute-start | bytes 6291464 | tf_op jit(solution)/shard_map/ppermute | solution.py:45
  152.1 83.3 %copy-start.7 = (bf16[1024,512]{1,0:T(8,128)(2,1)}, bf16[1024,512]{1,0:T(8,128)(2,1)S(1)}, u32[]{:S(2)}) copy-start(bf16[1024,512]{1,0:T(8,128)(2,1)S(1)} %collective-permute-done.20.refs_12_.refs_8_) | copy-start | bytes 3145732
  152.1 31.9 %collective-permute-start.21 = (bf16[1024,512]{1,0:T(8,128)(2,1)S(1)}, bf16[1024,512]{1,0:T(8,128)(2,1)S(1)}, u32[]{:S(2)}, u32[]{:S(2)}) collective-permute-start(bf16[1024,512]{1,0:T(8,128)(2,1)S(1)} %constant_dynamic-update-slice_fusion.2.refs_11_.refs_7_), channel_id=1, source_target_pairs={{0,1},{1,2},{2,3},{3,0},{4,5},{5,6},{6,7},{7,4},{8,11},{9,8},{10,9... | collective-permute-start | bytes 3145736 | tf_op jit(solution)/shard_map/ppermute | solution.py:45
  153.0 31.0 %collective-permute-start.23 = (bf16[1024,512]{1,0:T(8,128)(2,1)}, bf16[1024,512]{1,0:T(8,128)(2,1)S(1)}, u32[]{:S(2)}, u32[]{:S(2)}) collective-permute-start(bf16[1024,512]{1,0:T(8,128)(2,1)} %collective-permute-done.17.refs_5_.refs_9_), channel_id=1, source_target_pairs={{0,1},{1,2},{2,3},{3,0},{4,5},{5,6},{6,7},{7,4},{8,11},{9,8},{10,9... | collective-permute-start | bytes 3145736 | tf_op jit(solution)/shard_map/ppermute | solution.py:45
  184.0 64.0 %copy-start.8 = (bf16[1024,512]{1,0:T(8,128)(2,1)}, bf16[1024,512]{1,0:T(8,128)(2,1)S(1)}, u32[]{:S(2)}) copy-start(bf16[1024,512]{1,0:T(8,128)(2,1)S(1)} %collective-permute-done.21.refs_12_.refs_8_) | copy-start | bytes 3145732
  184.0 35.7 %collective-permute-start.22 = (bf16[256,4096]{1,0:T(8,128)(2,1)S(1)}, bf16[256,4096]{1,0:T(8,128)(2,1)S(1)}, u32[]{:S(2)}, u32[]{:S(2)}) collective-permute-start(bf16[256,4096]{1,0:T(8,128)(2,1)S(1)} %collective-permute-done.12), channel_id=1, source_target_pairs={{0,80},{1,81},{2,82},{3,83},{4,84},{5,85},{6,86},{7,87},{8,56},{9,... | collective-permute-start | bytes 6291464 | tf_op jit(solution)/shard_map/ppermute | solution.py:45
  184.1 35.7 %copy-start.10 = (bf16[1024,512]{1,0:T(8,128)(2,1)}, bf16[1024,512]{1,0:T(8,128)(2,1)S(1)}, u32[]{:S(2)}) copy-start(bf16[1024,512]{1,0:T(8,128)(2,1)S(1)} %collective-permute-done.23.refs_6_.refs_10_) | copy-start | bytes 3145732
  194.6 14.0 %collective-permute-start.28 = (bf16[1024,512]{1,0:T(8,128)(2,1)S(1)}, bf16[1024,512]{1,0:T(8,128)(2,1)}, u32[]{:S(2)}, u32[]{:S(2)}) collective-permute-start(bf16[1024,512]{1,0:T(8,128)(2,1)S(1)} %collective-permute-done.20.refs_12_.refs_8_), channel_id=1, source_target_pairs={{0,1},{1,2},{2,3},{3,0},{4,5},{5,6},{6,7},{7,4},{8,11},{9,8},{10,9... | collective-permute-start | bytes 3145736 | tf_op jit(solution)/shard_map/ppermute | solution.py:45
  196.4 23.3 %collective-permute-start.24 = (bf16[1024,512]{1,0:T(8,128)(2,1)S(1)}, bf16[1024,512]{1,0:T(8,128)(2,1)S(1)}, u32[]{:S(2)}, u32[]{:S(2)}) collective-permute-start(bf16[1024,512]{1,0:T(8,128)(2,1)S(1)} %collective-permute-done.21.refs_12_.refs_8_), channel_id=1, source_target_pairs={{0,1},{1,2},{2,3},{3,0},{4,5},{5,6},{6,7},{7,4},{8,11},{9,8},{10,9... | collective-permute-start | bytes 3145736 | tf_op jit(solution)/shard_map/ppermute | solution.py:45
  208.7 24.0 %collective-permute-start.29 = (bf16[1024,512]{1,0:T(8,128)(2,1)}, bf16[1024,512]{1,0:T(8,128)(2,1)}, u32[]{:S(2)}, u32[]{:S(2)}) collective-permute-start(bf16[1024,512]{1,0:T(8,128)(2,1)} %collective-permute-done.28.refs_13_.refs_9_), channel_id=1, source_target_pairs={{0,1},{1,2},{2,3},{3,0},{4,5},{5,6},{6,7},{7,4},{8,11},{9,8},{10,9... | collective-permute-start | bytes 3145736 | tf_op jit(solution)/shard_map/ppermute | solution.py:45
  211.6 82.4 %collective-permute-start.37 = (bf16[4096,512]{1,0:T(8,128)(2,1)}, bf16[4096,512]{1,0:T(8,128)(2,1)}, u32[]{:S(2)}, u32[]{:S(2)}) collective-permute-start(bf16[4096,512]{1,0:T(8,128)(2,1)} %get-tuple-element.101.refs_11_.refs_0_), channel_id=1, source_target_pairs={{0,8},{1,9},{2,10},{3,11},{4,12},{5,13},{6,14},{7,15},{8,0},{9,1},... | collective-permute-start | bytes 12582920 | tf_op jit(solution)/shard_map/ppermute | solution.py:45
  219.8 28.3 %copy-start.9 = (bf16[1024,512]{1,0:T(8,128)(2,1)}, bf16[1024,512]{1,0:T(8,128)(2,1)S(1)}, u32[]{:S(2)}) copy-start(bf16[1024,512]{1,0:T(8,128)(2,1)S(1)} %collective-permute-done.24.refs_13_.refs_9_) | copy-start | bytes 3145732
  227.5 6.9 %collective-permute-start.26 = (f32[256,640]{1,0:T(8,128)}, f32[256,640]{1,0:T(8,128)S(1)}, u32[]{:S(2)}, u32[]{:S(2)}) collective-permute-start(f32[256,640]{1,0:T(8,128)} %get-tuple-element.84.refs_3_), channel_id=1, source_target_pairs={{0,8},{1,9},{2,10},{3,11},{4,12},{5,13},{6,14},{7,15},{8,0},{9,1},... | collective-permute-start | bytes 1966088 | tf_op jit(solution)/shard_map/ppermute | solution.py:45
  232.5 2.9 collective-permute-start.27
  232.6 26.6 %collective-permute-start.32 = (bf16[1024,512]{1,0:T(8,128)(2,1)S(1)}, bf16[1024,512]{1,0:T(8,128)(2,1)S(1)}, u32[]{:S(2)}, u32[]{:S(2)}) collective-permute-start(bf16[1024,512]{1,0:T(8,128)(2,1)S(1)} %collective-permute-done.24.refs_13_.refs_9_), channel_id=1, source_target_pairs={{0,1},{1,2},{2,3},{3,0},{4,5},{5,6},{6,7},{7,4},{8,11},{9,8},{10,9... | collective-permute-start | bytes 3145736 | tf_op jit(solution)/shard_map/ppermute | solution.py:45
  248.1 11.1 %collective-permute-start.30 = (f32[256,640]{1,0:T(8,128)}, f32[256,640]{1,0:T(8,128)S(1)}, u32[]{:S(2)}, u32[]{:S(2)}) collective-permute-start(f32[256,640]{1,0:T(8,128)} %get-tuple-element.90.refs_3_), channel_id=1, source_target_pairs={{0,8},{1,9},{2,10},{3,11},{4,12},{5,13},{6,14},{7,15},{8,0},{9,1},... | collective-permute-start | bytes 1966088 | tf_op jit(solution)/shard_map/ppermute | solution.py:45
  249.6 11.5 %collective-permute-start.31 = (f32[256,640]{1,0:T(8,128)}, f32[256,640]{1,0:T(8,128)S(1)}, u32[]{:S(2)}, u32[]{:S(2)}) collective-permute-start(f32[256,640]{1,0:T(8,128)} %get-tuple-element.91.refs_4_), channel_id=1, source_target_pairs={{0,8},{1,9},{2,10},{3,11},{4,12},{5,13},{6,14},{7,15},{8,0},{9,1},... | collective-permute-start | bytes 1966088 | tf_op jit(solution)/shard_map/ppermute | solution.py:45
  273.8 2.4 collective-permute-start.33
  274.3 2.9 collective-permute-start.34
  288.6 5.4 %collective-permute-start.35 = (bf16[256,4096]{1,0:T(8,128)(2,1)}, bf16[256,4096]{1,0:T(8,128)(2,1)S(1)}, u32[]{:S(2)}, u32[]{:S(2)}) collective-permute-start(bf16[256,4096]{1,0:T(8,128)(2,1)} %get-tuple-element.99), channel_id=1, source_target_pairs={{0,8},{1,9},{2,10},{3,11},{4,12},{5,13},{6,14},{7,15},{8,0},{9,1},... | collective-permute-start | bytes 6291464 | tf_op jit(solution)/shard_map/ppermute | solution.py:45
  289.1 4.9 %collective-permute-start.36 = (f32[256,640]{1,0:T(8,128)}, f32[256,640]{1,0:T(8,128)S(1)}, u32[]{:S(2)}, u32[]{:S(2)}) collective-permute-start(f32[256,640]{1,0:T(8,128)} %get-tuple-element.100.mine), channel_id=1, source_target_pairs={{0,8},{1,9},{2,10},{3,11},{4,12},{5,13},{6,14},{7,15},{8,0},{9,1},... | collective-permute-start | bytes 1966088 | tf_op jit(solution)/shard_map/ppermute | solution.py:45
  (19 other events, 121.9 us)
